TPU v7x, 128 devices: a whole 4x4x4 slice. The times are simulated.
128 devices in a mesh: grp: 4 (over x_lo, core), slab: 32 (over y, z, x_hi).
Axes of the slice: x: 4 (x_hi: 2, x_lo: 2; x = x_hi * 2 + x_lo), y: 4, z: 4, core: 2. Of those that a mesh axis runs over, the one named last changes fastest.
Arguments:
- states: bfloat16 [128, 1024, 4096], P('grp', 'slab'), may hold values from -6 to 6
- core_density: float32 [1024, 4096], P('slab'), may hold values from 0.0015 to 0.032
- occupancy: int32 [128], P('grp'), may hold values from 1 to 8
Outputs:
- applied: bfloat16 [128, 1024, 4096], P('grp', 'slab')
- potential: float32 [1024, 4096], P('slab')
All inputs are finite; a program needn't handle non-finite values.
Results may differ from a plain program's by a relative error of at most 0.005.
Values sent between devices are 32-bit elements; how exact they have to be, the bound alone decides.
A program may use at most 128 MiB of HBM per device.

v0:
```python
import math

import jax
import jax.numpy as jnp
from jax import lax
from jax.sharding import PartitionSpec as P

NX = 64
NY = 64
OCC_DEN = 8


grid_step = 0.5
valence_norm = 0.04


def padded_2(cells, sides, width):
    for axis, dim in sides:
        count = lax.axis_size(axis)
        head = lax.slice_in_dim(cells, 0, width, axis=dim)
        tail = lax.slice_in_dim(cells, cells.shape[dim] - width, cells.shape[dim], axis=dim)
        cells = jnp.concatenate(
            [
                lax.ppermute(tail, axis, [(i, (i + 1) % count) for i in range(count)]),
                cells,
                lax.ppermute(head, axis, [((i + 1) % count, i) for i in range(count)]),
            ],
            axis=dim,
        )
    return cells


def energy(dens, sig):
    unif = -0.75 * (3.0 / math.pi) ** (1.0 / 3.0) * dens ** (4.0 / 3.0)
    reduced = sig / (4.0 * (3.0 * math.pi**2) ** (2.0 / 3.0) * dens ** (8.0 / 3.0))
    enhance = 1.0 + 0.804 - 0.804 / (1.0 + 0.2195149727645171 * reduced / 0.804)
    return unif * enhance


def total_energy(dens, sig):
    return jnp.sum(energy(dens, sig))


def trim(field, axis, active):
    if active:
        return lax.slice_in_dim(field, 2, field.shape[axis] - 2, axis=axis)
    return field


def slope(field, axis, padded):
    if padded:
        length = field.shape[axis]
        first = lax.slice_in_dim(field, 0, length - 4, axis=axis)
        second = lax.slice_in_dim(field, 1, length - 3, axis=axis)
        third = lax.slice_in_dim(field, 3, length - 1, axis=axis)
        fourth_part = lax.slice_in_dim(field, 4, length, axis=axis)
    else:
        first = jnp.roll(field, 2, axis)
        second = jnp.roll(field, 1, axis)
        third = jnp.roll(field, -1, axis)
        fourth_part = jnp.roll(field, -2, axis)
    return (first - 8.0 * second + 8.0 * third - fourth_part) / (12.0 * grid_step)


def body(states, core_density, occupancy):
    s_dev, planes, cells = states.shape
    groups = lax.axis_size("grp")
    weight = valence_norm * occupancy.astype(jnp.float32) / (OCC_DEN * s_dev * groups)
    wide = states.astype(jnp.float32)
    partial_value = jnp.einsum("s,szc->zc", weight, wide * wide).reshape(planes, NX, NY)
    core_grid = core_density.reshape(planes, NX, NY)
    width = 2
    density = core_grid + lax.psum(partial_value, "grp")
    extended = padded_2(density, (("slab", 0),), width)
    grad_z = trim(slope(extended, 0, True), 1, False)
    grad_x = trim(slope(extended, 1, False), 0, True)
    grad_y = trim(trim(slope(extended, 2, False), 0, True), 1, False)
    centre = trim(trim(extended, 0, True), 1, False)
    sigma = grad_x * grad_x + grad_y * grad_y + grad_z * grad_z
    d_dens, d_sig = jax.grad(total_energy, (0, 1))(centre, sigma)
    flow_z = 2.0 * d_sig * grad_z
    flow_x = 2.0 * d_sig * grad_x
    flow_y = 2.0 * d_sig * grad_y
    flow_z = padded_2(flow_z, (("slab", 0),), 2)
    d_dens = trim(trim(d_dens, 0, False), 1, False)
    div_z = trim(slope(flow_z, 0, True), 1, False)
    div_x = trim(slope(flow_x, 1, False), 0, False)
    div_y = trim(trim(slope(flow_y, 2, False), 0, False), 1, False)
    divergence = div_x + div_y + div_z
    potential = d_dens - divergence
    potential = potential.reshape(planes, cells)
    applied = (potential[None] * wide).astype(jnp.bfloat16)
    return (applied, potential)


def solution(mesh):
    placed = (P("grp", "slab", None), P("slab", None), P("grp"))
    return jax.shard_map(
        body,
        mesh=mesh,
        in_specs=placed,
        out_specs=(P("grp", "slab", None), P("slab", None)),
        check_vma=False,
    )
```

profile of v0, /device:TPU:1, one launch (start us, length us, event | category | flops | bytes accessed | tf_op | source)
XLA Modules:
  0.0 128.9 jit_solution(13817157214727536819)
XLA Ops:
  7.2 0.0 copy-start.2
  7.2 0.0 all-reduce.2.cloned.1.call-start
  7.2 9.4 %convert_multiply_fusion.1 = bf16[32,32,4096]{2,1,0:T(8,128)(2,1)} fusion(bf16[32,32,4096]{2,1,0:T(8,128)(2,1)} %param.3), kind=kLoop, calls=%fused_computation.1 | loop fusion | flops 12582912 | bytes 16777216 | tf_op jit(solution)/shard_map/mul | solution.py:70
  16.6 0.0 copy-done.2
  16.6 12.4 %fusion.1 = f32[1,32,4096]{2,0,1:T(1,128)S(1)} fusion(bf16[32,32,4096]{2,1,0:T(8,128)(2,1)} %convert_multiply_fusion.1, s32[32]{0:T(128)S(1)} %copy-done.2), kind=kOutput, calls=%fused_computation.3 | convolution fusion | flops 8388672 | bytes 8913024 | tf_op jit(solution)/shard_map/s,szc->zc/dot_general | solution.py:70
  29.0 0.3 copy.10
  29.3 0.0 copy-start.1
  29.4 1.4 %reshape.13 = f32[32,64,64]{2,1,0:T(8,128)} reshape(f32[32,4096]{1,0:T(8,128)S(1)} %bitcast.6) | data formatting | bytes 1048576 | tf_op jit(solution)/shard_map/reshape | solution.py:70
  30.7 0.0 all-reduce.2.cloned.1.call-update
  30.8 0.0 copy-done.1
  30.8 0.6 reshape.12
  31.4 44.4 %all-reduce.2.cloned.1.call-done = f32[32,64,64]{2,1,0:T(8,128)} async-done(((f32[32,64,64]{2,1,0:T(8,128)}), f32[32,64,64]{2,1,0:T(8,128)}) %all-reduce.2.cloned.1.call-update) | async-done | bytes 524304 | tf_op jit(solution)/shard_map/psum | solution.py:73
  75.8 1.4 %add.38 = f32[32,64,64]{2,1,0:T(8,128)S(1)} add(f32[32,64,64]{2,1,0:T(8,128)S(1)} %reshape.12, f32[32,64,64]{2,1,0:T(8,128)} %all-reduce.2.cloned.1.call-done) | non-fusion elementwise | flops 131072 | bytes 1572864 | tf_op jit(solution)/shard_map/add | solution.py:73
  77.2 2.5 %collective-permute-start = (f32[2,64,64]{2,1,0:T(8,128)S(1)}, f32[2,64,64]{2,1,0:T(8,128)S(1)}, u32[]{:S(2)}, u32[]{:S(2)}) collective-permute-start(f32[2,64,64]{2,1,0:T(8,128)S(1)} %get-tuple-element.41), channel_id=1, source_target_pairs={{0,1},{1,2},{2,3},{3,4},{4,5},{5,6},{6,7},{7,8},{8,9},{9,10},{10,1... | collective-permute-start | bytes 98312 | tf_op jit(solution)/shard_map/ppermute | solution.py:24
  79.7 4.8 %collective-permute-start.1 = (f32[2,64,64]{2,1,0:T(8,128)S(1)}, f32[2,64,64]{2,1,0:T(8,128)S(1)}, u32[]{:S(2)}, u32[]{:S(2)}) collective-permute-start(f32[2,64,64]{2,1,0:T(8,128)S(1)} %get-tuple-element.42), channel_id=1, source_target_pairs={{1,0},{2,1},{3,2},{4,3},{5,4},{6,5},{7,6},{8,7},{9,8},{10,9},{11,1... | collective-permute-start | bytes 98312 | tf_op jit(solution)/shard_map/ppermute | solution.py:26
  84.4 1.6 %collective-permute-done = f32[2,64,64]{2,1,0:T(8,128)S(1)} collective-permute-done((f32[2,64,64]{2,1,0:T(8,128)S(1)}, f32[2,64,64]{2,1,0:T(8,128)S(1)}, u32[]{:S(2)}, u32[]{:S(2)}) %collective-permute-start) | collective-permute-done | bytes 32800 | tf_op jit(solution)/shard_map/ppermute | solution.py:24
  86.1 0.0 collective-permute-done.1
  86.1 0.2 pad_maximum_fusion
  86.3 0.4 fusion.54
  86.8 0.4 fusion.53
  87.2 0.2 fusion.58
  87.4 0.4 fusion.55
  87.9 0.2 fusion.57
  88.1 0.4 fusion.56
  88.6 5.8 %fusion.49 = (f32[32,64,64]{2,1,0:T(8,128)S(1)}, f32[32,64,64]{2,1,0:T(8,128)S(1)}, f32[32,64,64]{2,1,0:T(8,128)S(1)}, f32[32,64,64]{2,1,0:T(8,128)S(1)}, f32[32,64,64]{2,1,0:T(8,128)S(1)}) fusion(f32[32,64,64]{2,1,0:T(8,128)S(1)} %add.38, f32[2,64,64]{2,1,0:T(8,128)S(1)} %collective-permute-done.1, f32[2,64,64]{2,1,0:T(8,128)S(1)} %collective-permute-done, ...), kind=kLoop, calls=%fused_computation.90 | loop fusion | flops 7340032 | bytes 8398848 | tf_op jit(solution)/shard_map/mul | solution.py:83
  94.4 0.3 fusion.67
  94.7 0.2 fusion.63
  95.0 0.2 fusion.65
  95.2 0.4 fusion.60
  95.6 0.4 fusion.59
  96.0 0.4 fusion.62
  96.3 0.4 fusion.61
  96.7 0.7 collective-permute-start.2
  97.5 6.8 %collective-permute-start.3 = (f32[2,64,64]{2,1,0:T(8,128)S(1)}, f32[2,64,64]{2,1,0:T(8,128)S(1)}, u32[]{:S(2)}, u32[]{:S(2)}) collective-permute-start(f32[2,64,64]{2,1,0:T(8,128)S(1)} %get-tuple-element.40), channel_id=1, source_target_pairs={{1,0},{2,1},{3,2},{4,3},{5,4},{6,5},{7,6},{8,7},{9,8},{10,9},{11,1... | collective-permute-start | bytes 98312 | tf_op jit(solution)/shard_map/ppermute | solution.py:26
  104.3 1.3 %collective-permute-done.2 = f32[2,64,64]{2,1,0:T(8,128)S(1)} collective-permute-done((f32[2,64,64]{2,1,0:T(8,128)S(1)}, f32[2,64,64]{2,1,0:T(8,128)S(1)}, u32[]{:S(2)}, u32[]{:S(2)}) %collective-permute-start.2) | collective-permute-done | bytes 32800 | tf_op jit(solution)/shard_map/ppermute | solution.py:24
  105.7 0.0 collective-permute-done.3
  105.7 6.3 %fusion.9 = f32[32,64,64]{2,1,0:T(8,128)S(1)} fusion(f32[32,64,64]{2,1,0:T(8,128)S(1)} %get-tuple-element.38, f32[2,64,64]{2,1,0:T(8,128)S(1)} %collective-permute-done.3, f32[2,64,64]{2,1,0:T(8,128)S(1)} %collective-permute-done.2, f32[32,62,64]{2,1,0:T(8,128)S(1)} %get-tuple-element.30, f32[32,2,64]{2,1,0:T(2,128)S(1)} %get-tuple-element.32, ...), kind=kLoop, calls=%fused_computation.26 | loop fusion | flops 8126464 | bytes 7405568 | tf_op jit(solution)/shard_map/sub | solution.py:90
  112.0 0.4 mul.155
  112.3 0.0 copy-start
  112.3 9.7 %fusion = bf16[32,32,4096]{2,1,0:T(8,128)(2,1)} fusion(bf16[32,32,4096]{2,1,0:T(8,128)(2,1)} %param.3, f32[32,4096]{1,0:T(8,128)S(1)} %mul.155), kind=kLoop, calls=%fused_computation.2 | loop fusion | flops 12582912 | bytes 17301504 | tf_op jit(solution)/shard_map/convert_element_type | solution.py:92
  122.0 0.0 copy-done
  (4 shorter events, 0.1 us)
Async XLA Ops:
  7.2 9.4 %copy-start.2 = (s32[32]{0:T(128)S(1)}, s32[32]{0:T(128)}, u32[]{:S(2)}) copy-start(s32[32]{0:T(128)} %param.5) | copy-start | bytes 388
  7.2 68.6 %all-reduce.2.cloned.1.call-start = ((), (), s32[]{:S(2)}) async-start(), calls=%async_computation | async-start | bytes 2097152 | tf_op jit(solution)/shard_map/psum | solution.py:73
  29.3 1.4 %copy-start.1 = (f32[32,4096]{1,0:T(8,128)S(1)}, f32[32,4096]{1,0:T(8,128)}, u32[]{:S(2)}) copy-start(f32[32,4096]{1,0:T(8,128)} %param.4) | copy-start | bytes 1572868
  77.2 8.9 %collective-permute-start = (f32[2,64,64]{2,1,0:T(8,128)S(1)}, f32[2,64,64]{2,1,0:T(8,128)S(1)}, u32[]{:S(2)}, u32[]{:S(2)}) collective-permute-start(f32[2,64,64]{2,1,0:T(8,128)S(1)} %get-tuple-element.41), channel_id=1, source_target_pairs={{0,1},{1,2},{2,3},{3,4},{4,5},{5,6},{6,7},{7,8},{8,9},{9,10},{10,1... | collective-permute-start | bytes 98312 | tf_op jit(solution)/shard_map/ppermute | solution.py:24
  79.7 6.4 %collective-permute-start.1 = (f32[2,64,64]{2,1,0:T(8,128)S(1)}, f32[2,64,64]{2,1,0:T(8,128)S(1)}, u32[]{:S(2)}, u32[]{:S(2)}) collective-permute-start(f32[2,64,64]{2,1,0:T(8,128)S(1)} %get-tuple-element.42), channel_id=1, source_target_pairs={{1,0},{2,1},{3,2},{4,3},{5,4},{6,5},{7,6},{8,7},{9,8},{10,9},{11,1... | collective-permute-start | bytes 98312 | tf_op jit(solution)/shard_map/ppermute | solution.py:26
  96.7 8.9 %collective-permute-start.2 = (f32[2,64,64]{2,1,0:T(8,128)S(1)}, f32[2,64,64]{2,1,0:T(8,128)S(1)}, u32[]{:S(2)}, u32[]{:S(2)}) collective-permute-start(f32[2,64,64]{2,1,0:T(8,128)S(1)} %get-tuple-element.39), channel_id=1, source_target_pairs={{0,1},{1,2},{2,3},{3,4},{4,5},{5,6},{6,7},{7,8},{8,9},{9,10},{10,1... | collective-permute-start | bytes 98312 | tf_op jit(solution)/shard_map/ppermute | solution.py:24
  97.5 8.2 %collective-permute-start.3 = (f32[2,64,64]{2,1,0:T(8,128)S(1)}, f32[2,64,64]{2,1,0:T(8,128)S(1)}, u32[]{:S(2)}, u32[]{:S(2)}) collective-permute-start(f32[2,64,64]{2,1,0:T(8,128)S(1)} %get-tuple-element.40), channel_id=1, source_target_pairs={{1,0},{2,1},{3,2},{4,3},{5,4},{6,5},{7,6},{8,7},{9,8},{10,9},{11,1... | collective-permute-start | bytes 98312 | tf_op jit(solution)/shard_map/ppermute | solution.py:26
  112.3 9.7 %copy-start = (f32[32,4096]{1,0:T(8,128)}, f32[32,4096]{1,0:T(8,128)S(1)}, u32[]{:S(2)}) copy-start(f32[32,4096]{1,0:T(8,128)S(1)} %mul.155) | copy-start | bytes 1572868
Sparse Core Ops, SparseCore 0:
  30.9 44.8 all-reduce.1
where the time goes:
time: 130 us; the launch traced here: 129 us
  waiting for transfers between devices  47.4 us (36%)
  other arithmetic  33.1 us (25%)
  starting transfers between devices  14.9 us (11%)
  between operations  14.2 us (11%)
  matrix products  12.4 us (10%)
  local copies, waits for them, and re-layouts  6.87 us (5%)
    psum x1, waiting for transfers between devices, body(): density = core_grid + lax.psum(partial_value, 'grp')  44.4 us
    dot_general x1, matrix products, body(): jnp.einsum('s,szc->zc', weight, wide * wide).reshape(planes, NX, NY)  12.4 us
    ppermute x2, starting transfers between devices, padded_2(): lax.ppermute(head, axis, [((i + 1) % count, i) for i in range(count)])  11.6 us
    convert_element_type x1, other arithmetic, body(): applied = (potential[None] * wide).astype(jnp.bfloat16)  9.68 us
    mul x1, other arithmetic, body(): wide * wide  9.38 us
    sub x1, other arithmetic, body(): potential = d_dens - divergence  6.3 us
    mul x1, other arithmetic, body(): flow_y = 2.0 * d_sig * grad_y  5.84 us
    ppermute x2, starting transfers between devices, padded_2(): lax.ppermute(tail, axis, [(i, (i + 1) % count) for i in range(count)])  3.2 us
  transfers between devices with their start and end apart: 5, of which 3 were waited for; matrix products, arithmetic and copies ran while one was open for 0% of the time, Pallas kernels for 0%

commit v1 on v0

v1 whole, which is shorter than its diff:
```python
import functools
import math

import jax
import jax.numpy as jnp
from jax import lax
from jax.experimental import pallas as pl
from jax.experimental.pallas import tpu as pltpu
from jax.sharding import PartitionSpec as P

MESH = pl.DeviceIdType.MESH

NX = 64
NY = 64
OCC_DEN = 8
LANES = 128

grid_step = 0.5
valence_norm = 0.04

kappa = 0.804
mu = 0.2195149727645171
exchange = -0.75 * (3.0 / math.pi) ** (1.0 / 3.0)
reduced_scale = 4.0 * (3.0 * math.pi**2) ** (2.0 / 3.0)
stencil_scale = 1.0 / (12.0 * grid_step)
u_scale = mu / kappa / reduced_scale * stencil_scale * stencil_scale
flow_scale = 2.0 * exchange * mu / reduced_scale * stencil_scale * stencil_scale
slope_scale = exchange * 4.0 / 3.0

CHUNKS = 8


def stencil(before2, before1, after1, after2):
    return (before2 - after2) + 8.0 * (after1 - before1)


def swap_halves(tile):
    return pltpu.roll(tile, 64, 1)


def along_y(tile, swapped, inner):
    before2 = pltpu.roll(jnp.where(inner >= NY - 2, swapped, tile), 2, 1)
    before1 = pltpu.roll(jnp.where(inner >= NY - 1, swapped, tile), 1, 1)
    after1 = pltpu.roll(jnp.where(inner < 1, swapped, tile), LANES - 1, 1)
    after2 = pltpu.roll(jnp.where(inner < 2, swapped, tile), LANES - 2, 1)
    return stencil(before2, before1, after1, after2)


def along_x(left, left_swapped, swapped, right, right_swapped, low):
    before1 = jnp.where(low, left_swapped, swapped)
    after1 = jnp.where(low, swapped, right_swapped)
    return stencil(left, before1, after1, right)


def along_z(tile):
    rows = tile.shape[0]
    return stencil(
        pltpu.roll(tile, 2, 0),
        pltpu.roll(tile, 1, 0),
        pltpu.roll(tile, rows - 1, 0),
        pltpu.roll(tile, rows - 2, 0),
    )


def potential_kernel(
    slabs,
    occ_ref,
    states_ref,
    core_ref,
    held_ref,
    pot_ref,
    part,
    from_core,
    chip_sum,
    from_chip,
    core_half,
    dens,
    above,
    below,
    flow_x,
    local,
    load_sem,
    core_sem,
    core_send,
    core_recv,
    chip_send,
    chip_recv,
    up_send,
    up_recv,
    down_send,
    down_recv,
    pot_send,
    pot_recv,
):
    s_dev, planes, cells = states_ref.shape
    half = planes // 2
    width = cells // CHUNKS
    tiles = width // LANES
    n_tiles = cells // LANES

    grp = lax.axis_index("grp")
    slab = lax.axis_index("slab")
    chip = grp // 2
    core = grp % 2
    core_peer = {"grp": chip * 2 + 1 - core, "slab": slab}
    chip_peer = {"grp": (1 - chip) * 2 + core, "slab": slab}
    up_peer = {
        "grp": (chip * (1 - core) + (1 - chip) * core) * 2 + 1 - core,
        "slab": (slab + core) % slabs,
    }
    down_peer = {
        "grp": (chip * core + (1 - chip) * (1 - core)) * 2 + 1 - core,
        "slab": (slab + slabs - 1 + core) % slabs,
    }
    slab_peer = {
        "grp": (1 - chip) * 2 + 1 - core,
        "slab": (slab + slabs - 1 + 2 * core) % slabs,
    }

    def cols(i):
        return pl.ds(pl.multiple_of(i * width, LANES), width)

    def load(i):
        return pltpu.make_async_copy(
            states_ref.at[:, :, cols(i)], held_ref.at[:, :, cols(i)], load_sem.at[i]
        )

    def remote(src, dst, send, recv, peer, i):
        return pltpu.make_async_remote_copy(
            src_ref=src,
            dst_ref=dst,
            send_sem=send.at[i],
            recv_sem=recv.at[i],
            device_id=peer,
            device_id_type=MESH,
        )

    def to_core(i):
        return remote(
            part.at[1 - core, :, cols(i)], from_core.at[:, cols(i)], core_send, core_recv, core_peer, i
        )

    def to_chip(i):
        return remote(chip_sum.at[:, cols(i)], from_chip.at[:, cols(i)], chip_send, chip_recv, chip_peer, i)

    def to_up(i):
        return remote(dens.at[pl.ds(half - 8, 8), cols(i)], below.at[:, cols(i)], up_send, up_recv, up_peer, i)

    def to_down(i):
        return remote(dens.at[pl.ds(0, 8), cols(i)], above.at[:, cols(i)], down_send, down_recv, down_peer, i)

    def own_rows():
        return pl.ds(pl.multiple_of(core * half, half), half)

    def to_pot(i):
        where = pot_ref.at[own_rows(), cols(i)]
        return remote(where, where, pot_send, pot_recv, core_peer, i)

    core_copy = pltpu.make_async_copy(core_ref.at[own_rows(), :], core_half, core_sem)
    for i in range(CHUNKS):
        load(i).start()
    core_copy.start()

    barrier = pltpu.get_barrier_semaphore()
    for peer in (core_peer, chip_peer, slab_peer):
        pl.semaphore_signal(barrier, inc=1, device_id=peer, device_id_type=MESH)

    weights = [
        occ_ref[s].astype(jnp.float32) * (valence_norm / (OCC_DEN * s_dev * 4))
        for s in range(s_dev)
    ]

    def density_part(i):
        def tile_step(t, carry):
            lanes = pl.ds(pl.multiple_of(i * width + t * LANES, LANES), LANES)
            total = jnp.zeros((planes, LANES), jnp.float32)
            for s in range(s_dev):
                wide = held_ref[s, :, lanes].astype(jnp.float32)
                total = total + (wide * weights[s]) * wide
            part[0, :, lanes] = total[:half]
            part[1, :, lanes] = total[half:]
            return carry

        lax.fori_loop(0, tiles, tile_step, 0)

    def chip_part(i):
        to_core(i).wait_recv()
        chip_sum[:, cols(i)] = part[core, :, cols(i)] + from_core[:, cols(i)]
        to_chip(i).start()

    for i in range(CHUNKS):
        load(i).wait()
        density_part(i)
        if i == 0:
            pl.semaphore_wait(barrier, 3)
        to_core(i).start()
        if i > 0:
            chip_part(i - 1)
    chip_part(CHUNKS - 1)
    core_copy.wait()

    lane = lax.broadcasted_iota(jnp.int32, (1, LANES), 1)
    inner = lane % NY
    low = lane < NY
    upper_row = lax.broadcasted_iota(jnp.int32, (8, LANES), 0) < 4

    def field(t):
        lanes = pl.ds(pl.multiple_of((t % n_tiles) * LANES, LANES), LANES)
        edge = jnp.where(upper_row, above[:, lanes], below[:, lanes])
        return jnp.concatenate([dens[:, lanes], edge], axis=0)

    def flow_step(t, carry):
        centre = field(t)
        left = field(t + n_tiles - 1)
        right = field(t + 1)
        swapped = swap_halves(centre)
        grad_x = along_x(left, swap_halves(left), swapped, right, swap_halves(right), low)
        grad_y = along_y(centre, swapped, inner)
        grad_z = along_z(centre)
        sigma = grad_x * grad_x + grad_y * grad_y + grad_z * grad_z
        root = jnp.exp2(jnp.log2(centre) * (-1.0 / 3.0))
        root2 = root * root
        root4 = root2 * root2
        share = 1.0 / (1.0 + u_scale * (sigma * (root4 * root4)))
        flow = flow_scale * (root4 * (share * share))
        d_dens = (slope_scale * (centre * root2)) * (
            (1.0 + kappa) + share * (2.0 * kappa * share - 3.0 * kappa)
        )
        flow_y = flow * grad_y
        div_y = along_y(flow_y[:half], swap_halves(flow_y[:half]), inner)
        div_z = along_z(flow * grad_z)[:half]
        lanes = pl.ds(pl.multiple_of((t % n_tiles) * LANES, LANES), LANES)
        flow_x[:, lanes] = (flow * grad_x)[:half]
        local[:, lanes] = d_dens[:half] - (div_y + div_z)
        return carry

    def pot_step(t, carry):
        def at(k):
            return flow_x[:, pl.ds(pl.multiple_of((k % n_tiles) * LANES, LANES), LANES)]

        lanes = pl.ds(pl.multiple_of((t % n_tiles) * LANES, LANES), LANES)
        left, centre, right = at(t + n_tiles - 1), at(t), at(t + 1)
        div_x = along_x(
            left, swap_halves(left), swap_halves(centre), right, swap_halves(right), low
        )
        pot_ref[own_rows(), lanes] = local[:, lanes] - div_x
        return carry

    for i in range(CHUNKS):
        to_chip(i).wait_recv()
        dens[:, cols(i)] = (chip_sum[:, cols(i)] + from_chip[:, cols(i)]) + core_half[:, cols(i)]
        to_up(i).start()
        to_down(i).start()

    for i in range(CHUNKS):
        to_up(i).wait_recv()
        to_down(i).wait_recv()

    lax.fori_loop(0, n_tiles, flow_step, 0)
    for i in range(CHUNKS):
        lax.fori_loop(i * tiles, (i + 1) * tiles, pot_step, 0)
        to_pot(i).start()
    for i in range(CHUNKS):
        to_core(i).wait_send()
        to_chip(i).wait_send()
        to_up(i).wait_send()
        to_down(i).wait_send()
        to_pot(i).wait()


def apply_kernel(held_ref, pot_ref, applied_ref, out_ref, staged, store_sem, pot_sem):
    s_dev, planes, cells = held_ref.shape
    width = cells // CHUNKS
    pot_copy = pltpu.make_async_copy(pot_ref, out_ref, pot_sem)
    pot_copy.start()

    def store(i):
        cols = pl.ds(i * width, width)
        return pltpu.make_async_copy(staged.at[:, :, cols], applied_ref.at[:, :, cols], store_sem.at[i])

    for i in range(CHUNKS):
        for t in range(width // LANES):
            lanes = pl.ds(i * width + t * LANES, LANES)
            pot = pot_ref[:, lanes]

            def state_step(s, carry):
                staged[s, :, lanes] = (held_ref[s, :, lanes].astype(jnp.float32) * pot).astype(jnp.bfloat16)
                return carry

            lax.fori_loop(0, s_dev, state_step, 0, unroll=8)
        store(i).start()
    for i in range(CHUNKS):
        store(i).wait()
    pot_copy.wait()


def body(slabs, states, core_density, occupancy):
    s_dev, planes, cells = states.shape
    half = planes // 2
    vmem = pl.BlockSpec(memory_space=pltpu.VMEM)
    anywhere = pl.BlockSpec(memory_space=pltpu.HBM)
    pair = pltpu.SemaphoreType.DMA((CHUNKS,))
    states = pltpu.with_memory_space_constraint(states, pltpu.HBM)
    core_density = pltpu.with_memory_space_constraint(core_density, pltpu.HBM)
    held, pot = pl.pallas_call(
        functools.partial(potential_kernel, slabs),
        out_shape=(
            pltpu.VMEM((s_dev, planes, cells), jnp.bfloat16),
            pltpu.VMEM((planes, cells), jnp.float32),
        ),
        in_specs=[pl.BlockSpec(memory_space=pltpu.SMEM), anywhere, anywhere],
        out_specs=(vmem, vmem),
        scratch_shapes=[
            pltpu.VMEM((2, half, cells), jnp.float32),
            pltpu.VMEM((half, cells), jnp.float32),
            pltpu.VMEM((half, cells), jnp.float32),
            pltpu.VMEM((half, cells), jnp.float32),
            pltpu.VMEM((half, cells), jnp.float32),
            pltpu.VMEM((half, cells), jnp.float32),
            pltpu.VMEM((8, cells), jnp.float32),
            pltpu.VMEM((8, cells), jnp.float32),
            pltpu.VMEM((half, cells), jnp.float32),
            pltpu.VMEM((half, cells), jnp.float32),
            pair,
            pltpu.SemaphoreType.DMA,
        ]
        + [pair] * 10,
        compiler_params=pltpu.CompilerParams(
            collective_id=0, has_side_effects=True, vmem_limit_bytes=24 * 1024 * 1024
        ),
        name="potential",
    )(occupancy, states, core_density)
    return pl.pallas_call(
        apply_kernel,
        out_shape=(
            jax.ShapeDtypeStruct((s_dev, planes, cells), jnp.bfloat16),
            jax.ShapeDtypeStruct((planes, cells), jnp.float32),
        ),
        in_specs=[vmem, vmem],
        out_specs=(anywhere, anywhere),
        scratch_shapes=[
            pltpu.VMEM((s_dev, planes, cells), jnp.bfloat16),
            pair,
            pltpu.SemaphoreType.DMA,
        ],
        compiler_params=pltpu.CompilerParams(vmem_limit_bytes=32 * 1024 * 1024),
        name="apply",
    )(held, pot)


def solution(mesh):
    placed = (P("grp", "slab", None), P("slab", None), P("grp"))
    return jax.shard_map(
        functools.partial(body, mesh.shape["slab"]),
        mesh=mesh,
        in_specs=placed,
        out_specs=(P("grp", "slab", None), P("slab", None)),
        check_vma=False,
    )
```

time: 130 us -> 42.4 us (0.33)
  waiting for transfers between devices: 47.4 us -> 0 us
  Pallas kernels: 0 us -> 41 us
  other arithmetic: 33.1 us -> 0 us
  starting transfers between devices: 14.9 us -> 0 us
  between operations: 14.2 us -> 0.65 us
  matrix products: 12.4 us -> 0 us
  local copies, waits for them, and re-layouts: 6.87 us -> 0.65 us
    psum x1 -> x0, waiting for transfers between devices: 44.4 us -> none  [body(): density = core_grid + lax.psum(partial_value, 'grp')]
    pallas_call x0 -> x2, Pallas kernels: none -> 41 us  [the longest x1 35.8 us: body(): pl.pallas_call(functools.partial(potential_kernel, slabs), out_shape=(plt...]
    mul x3 -> x0, other arithmetic: 15.5 us -> none  [the longest x1 9.38 us: body(): wide * wide]
    ppermute x4 -> x0, starting transfers between devices: 14.8 us -> none  [the longest x2 11.6 us: padded_2(): lax.ppermute(head, axis, [((i + 1) % count, i) for i in range(count)])]
    dot_general x1 -> x0, matrix products: 12.4 us -> none  [body(): jnp.einsum('s,szc->zc', weight, wide * wide).reshape(planes, NX, NY)]
    convert_element_type x1 -> x0, other arithmetic: 9.68 us -> none  [body(): applied = (potential[None] * wide).astype(jnp.bfloat16)]
    sub x1 -> x0, other arithmetic: 6.3 us -> none  [body(): potential = d_dens - divergence]
    slice x16 -> x0, local copies, waits for them, and re-layouts: 4.2 us -> none  [the longest x3 1.08 us: slope(): second = jnp.roll(field, 1, axis)]
  transfers between devices with their start and end apart: 5 -> 0, of which waited for: 3 -> 0; matrix products, arithmetic and copies ran while one was open for 0% -> 0% of each run, Pallas kernels for 0% -> 0%
where the time goes in v1:
time: 42.4 us; the launch traced here: 42.3 us
  Pallas kernels  41 us (97%)
  local copies, waits for them, and re-layouts  0.65 us (2%)
  between operations  0.65 us (2%)
    pallas_call x1, Pallas kernels, body(): pl.pallas_call(functools.partial(potential_kernel, slabs), out_shape=(plt...  35.8 us
    pallas_call x1, Pallas kernels, body(): pl.pallas_call(apply_kernel, out_shape=(jax.ShapeDtypeStruct((s_dev, plan...  5.24 us

profile of v1, /device:TPU:1, one launch (start us, length us, event | category | flops | bytes accessed | tf_op | source)
XLA Modules:
  0.0 42.3 jit_solution(7263729695487902202)
XLA Ops:
  0.6 0.0 copy-start
  0.6 0.6 %copy-done = s32[32]{0:T(128)S(1)} copy-done((s32[32]{0:T(128)S(1)}, s32[32]{0:T(128)}, u32[]{:S(2)}) %copy-start) | copy-done | bytes 152
  1.3 35.8 %potential.1 = (bf16[32,32,4096]{2,1,0:T(8,128)(2,1)S(1)}, f32[32,4096]{1,0:T(8,128)S(1)}) custom-call(s32[32]{0:T(128)S(1)} %copy-done, bf16[32,32,4096]{2,1,0:T(8,128)(2,1)} %states_ref.1, f32[32,4096]{1,0:T(8,128)} %core_ref.1), custom_call_target="tpu_custom_call" | custom-call | tf_op jit(solution)/shard_map/potential/pallas_call | solution.py:305
  37.1 5.2 %apply.1 = (bf16[32,32,4096]{2,1,0:T(8,128)(2,1)}, f32[32,4096]{1,0:T(8,128)}) custom-call(bf16[32,32,4096]{2,1,0:T(8,128)(2,1)S(1)} %get-tuple-element.4.held_ref, f32[32,4096]{1,0:T(8,128)S(1)} %get-tuple-element.5.pot_ref), custom_call_target="tpu_custom_call" | custom-call | tf_op jit(solution)/shard_map/apply/pallas_call | solution.py:333
Async XLA Ops:
  0.6 0.7 %copy-start = (s32[32]{0:T(128)S(1)}, s32[32]{0:T(128)}, u32[]{:S(2)}) copy-start(s32[32]{0:T(128)} %occ_ref.1) | copy-start | bytes 388

commit v2 on v1

--- a/solution.py
+++ b/solution.py
@@ -172,8 +172,8 @@
 
     def density_part(i):
         def tile_step(t, carry):
-            lanes = pl.ds(pl.multiple_of(i * width + t * LANES, LANES), LANES)
-            total = jnp.zeros((planes, LANES), jnp.float32)
+            lanes = pl.ds(pl.multiple_of(i * width + t * 2 * LANES, LANES), 2 * LANES)
+            total = jnp.zeros((planes, 2 * LANES), jnp.float32)
             for s in range(s_dev):
                 wide = held_ref[s, :, lanes].astype(jnp.float32)
                 total = total + (wide * weights[s]) * wide
@@ -181,7 +181,7 @@
             part[1, :, lanes] = total[half:]
             return carry
 
-        lax.fori_loop(0, tiles, tile_step, 0)
+        lax.fori_loop(0, tiles // 2, tile_step, 0)
 
     def chip_part(i):
         to_core(i).wait_recv()
@@ -256,9 +256,9 @@
         to_up(i).wait_recv()
         to_down(i).wait_recv()
 
-    lax.fori_loop(0, n_tiles, flow_step, 0)
-    for i in range(CHUNKS):
-        lax.fori_loop(i * tiles, (i + 1) * tiles, pot_step, 0)
+    lax.fori_loop(0, n_tiles, flow_step, 0, unroll=8)
+    for i in range(CHUNKS):
+        lax.fori_loop(i * tiles, (i + 1) * tiles, pot_step, 0, unroll=True)
         to_pot(i).start()
     for i in range(CHUNKS):
         to_core(i).wait_send()
@@ -279,15 +279,14 @@
         return pltpu.make_async_copy(staged.at[:, :, cols], applied_ref.at[:, :, cols], store_sem.at[i])
 
     for i in range(CHUNKS):
-        for t in range(width // LANES):
-            lanes = pl.ds(i * width + t * LANES, LANES)
-            pot = pot_ref[:, lanes]
-
-            def state_step(s, carry):
-                staged[s, :, lanes] = (held_ref[s, :, lanes].astype(jnp.float32) * pot).astype(jnp.bfloat16)
-                return carry
-
-            lax.fori_loop(0, s_dev, state_step, 0, unroll=8)
+        cols = pl.ds(i * width, width)
+        pot = pot_ref[:, cols].astype(jnp.bfloat16)
+
+        def state_step(s, carry):
+            staged[s, :, cols] = held_ref[s, :, cols] * pot
+            return carry
+
+        lax.fori_loop(0, s_dev, state_step, 0, unroll=8)
         store(i).start()
     for i in range(CHUNKS):
         store(i).wait()

time: 42.4 us -> 30.7 us (0.72)
  Pallas kernels: 41 us -> 29.2 us
    pallas_call x1, Pallas kernels: 35.8 us -> 25.7 us  [body(): pl.pallas_call(functools.partial(potential_kernel, slabs), out_shape=(plt...]
    pallas_call x1, Pallas kernels: 5.24 us -> 3.55 us  [body(): pl.pallas_call(apply_kernel, out_shape=(jax.ShapeDtypeStruct((s_dev, plan...]
where the time goes in v2:
time: 30.7 us; the launch traced here: 30.5 us
  Pallas kernels  29.2 us (95%)
  local copies, waits for them, and re-layouts  0.65 us (2%)
  between operations  0.65 us (2%)
    pallas_call x1, Pallas kernels, body(): pl.pallas_call(functools.partial(potential_kernel, slabs), out_shape=(plt...  25.7 us
    pallas_call x1, Pallas kernels, body(): pl.pallas_call(apply_kernel, out_shape=(jax.ShapeDtypeStruct((s_dev, plan...  3.55 us
    unnamed x2, local copies, waits for them, and re-layouts  0.65 us

profile of v2, /device:TPU:1, one launch (start us, length us, event | category | flops | bytes accessed | tf_op | source)
XLA Modules:
  0.0 30.5 jit_solution(5174992023680947298)
XLA Ops:
  0.6 0.0 copy-start
  0.6 0.6 %copy-done = s32[32]{0:T(128)S(1)} copy-done((s32[32]{0:T(128)S(1)}, s32[32]{0:T(128)}, u32[]{:S(2)}) %copy-start) | copy-done | bytes 152
  1.3 25.7 %potential.1 = (bf16[32,32,4096]{2,1,0:T(8,128)(2,1)S(1)}, f32[32,4096]{1,0:T(8,128)S(1)}) custom-call(s32[32]{0:T(128)S(1)} %copy-done, bf16[32,32,4096]{2,1,0:T(8,128)(2,1)} %states_ref.1, f32[32,4096]{1,0:T(8,128)} %core_ref.1), custom_call_target="tpu_custom_call" | custom-call | tf_op jit(solution)/shard_map/potential/pallas_call | solution.py:304
  27.0 3.6 %apply.1 = (bf16[32,32,4096]{2,1,0:T(8,128)(2,1)}, f32[32,4096]{1,0:T(8,128)}) custom-call(bf16[32,32,4096]{2,1,0:T(8,128)(2,1)S(1)} %get-tuple-element.4.held_ref, f32[32,4096]{1,0:T(8,128)S(1)} %get-tuple-element.5.pot_ref), custom_call_target="tpu_custom_call" | custom-call | tf_op jit(solution)/shard_map/apply/pallas_call | solution.py:332
Async XLA Ops:
  0.6 0.7 %copy-start = (s32[32]{0:T(128)S(1)}, s32[32]{0:T(128)}, u32[]{:S(2)}) copy-start(s32[32]{0:T(128)} %occ_ref.1) | copy-start | bytes 388

commit v3 on v2

v3 whole, which is shorter than its diff:
```python
import functools
import math

import jax
import jax.numpy as jnp
from jax import lax
from jax.experimental import pallas as pl
from jax.experimental.pallas import tpu as pltpu
from jax.sharding import PartitionSpec as P

MESH = pl.DeviceIdType.MESH

NX = 64
NY = 64
OCC_DEN = 8
LANES = 128

grid_step = 0.5
valence_norm = 0.04

kappa = 0.804
mu = 0.2195149727645171
exchange = -0.75 * (3.0 / math.pi) ** (1.0 / 3.0)
reduced_scale = 4.0 * (3.0 * math.pi**2) ** (2.0 / 3.0)
stencil_scale = 1.0 / (12.0 * grid_step)
u_scale = mu / kappa / reduced_scale * stencil_scale * stencil_scale
flow_scale = 2.0 * exchange * mu / reduced_scale * stencil_scale * stencil_scale
slope_scale = exchange * 4.0 / 3.0

CHUNKS = 4
STEP = 4 * LANES
STORES = 8


def stencil(before2, before1, after1, after2):
    return (before2 - after2) + 8.0 * (after1 - before1)


def swap_halves(tile):
    return pltpu.roll(tile, 64, 1)


def along_y(tile, swapped, inner):
    before2 = pltpu.roll(jnp.where(inner >= NY - 2, swapped, tile), 2, 1)
    before1 = pltpu.roll(jnp.where(inner >= NY - 1, swapped, tile), 1, 1)
    after1 = pltpu.roll(jnp.where(inner < 1, swapped, tile), LANES - 1, 1)
    after2 = pltpu.roll(jnp.where(inner < 2, swapped, tile), LANES - 2, 1)
    return stencil(before2, before1, after1, after2)


def along_x(left, left_swapped, swapped, right, right_swapped, low):
    before1 = jnp.where(low, left_swapped, swapped)
    after1 = jnp.where(low, swapped, right_swapped)
    return stencil(left, before1, after1, right)


def along_z(tile):
    rows = tile.shape[0]
    return stencil(
        pltpu.roll(tile, 2, 0),
        pltpu.roll(tile, 1, 0),
        pltpu.roll(tile, rows - 1, 0),
        pltpu.roll(tile, rows - 2, 0),
    )


def potential_kernel(
    slabs,
    occ_hbm,
    states_ref,
    core_ref,
    held_ref,
    pot_ref,
    occ_ref,
    part,
    from_core,
    chip_sum,
    from_chip,
    core_half,
    dens,
    inner_in,
    edge_out,
    edge_in,
    outer,
    flow_x,
    local,
    load_sem,
    misc_sem,
    group_sem,
    slab_sem,
    core_send,
    core_recv,
    chip_send,
    chip_recv,
    inner_send,
    inner_recv,
    edge_send,
    edge_recv,
    pot_send,
    pot_recv,
):
    s_dev, planes, cells = states_ref.shape
    half = planes // 2
    width = cells // CHUNKS
    n_tiles = cells // LANES

    grp = lax.axis_index("grp")
    slab = lax.axis_index("slab")
    chip = grp // 2
    core = grp % 2
    core_peer = {"grp": chip * 2 + 1 - core, "slab": slab}
    chip_peer = {"grp": (1 - chip) * 2 + core, "slab": slab}
    cross_peer = {"grp": (1 - chip) * 2 + 1 - core, "slab": slab}
    beyond = (slab + slabs - 1 + 2 * core) % slabs
    edge_chips = (chip, 1 - chip)

    def cols(i):
        return pl.ds(pl.multiple_of(i * width, LANES), width)

    def load(h, i):
        where = (slice(None), pl.ds(h * half, half), cols(i))
        return pltpu.make_async_copy(states_ref.at[where], held_ref.at[where], load_sem.at[h * CHUNKS + i])

    def remote(src, dst, send, recv, peer):
        return pltpu.make_async_remote_copy(
            src_ref=src, dst_ref=dst, send_sem=send, recv_sem=recv, device_id=peer, device_id_type=MESH
        )

    def to_core(i):
        return remote(
            part.at[1 - core, :, cols(i)], from_core.at[:, cols(i)], core_send.at[i], core_recv.at[i], core_peer
        )

    def to_chip(i):
        return remote(
            chip_sum.at[:, cols(i)], from_chip.at[:, cols(i)], chip_send.at[i], chip_recv.at[i], chip_peer
        )

    def to_edge(k):
        peer = {"grp": edge_chips[k] * 2 + 1 - core, "slab": beyond}
        return remote(edge_out, edge_in.at[chip], edge_send.at[k], edge_recv.at[chip], peer)

    def from_edge(k):
        return remote(edge_out, edge_in.at[k], edge_send.at[k], edge_recv.at[k], core_peer)

    def to_inner(i):
        rows = pl.ds(pl.multiple_of((1 - core) * 8, 8), 8)
        return remote(
            dens.at[rows, cols(i)], inner_in.at[:, cols(i)], inner_send.at[i], inner_recv.at[i], core_peer
        )

    def own_rows():
        return pl.ds(pl.multiple_of(core * half, half), half)

    def to_pot(i):
        where = pot_ref.at[own_rows(), cols(i)]
        return remote(where, where, pot_send.at[i], pot_recv.at[i], core_peer)

    occ_copy = pltpu.make_async_copy(occ_hbm, occ_ref, misc_sem.at[0])
    occ_copy.start()
    for h in (1, 0):
        for i in range(CHUNKS):
            load(h, i).start()
    core_copy = pltpu.make_async_copy(core_ref.at[own_rows(), :], core_half, misc_sem.at[1])
    core_copy.start()

    barrier = pltpu.get_barrier_semaphore()

    def greet(peer):
        pl.semaphore_signal(barrier, inc=1, device_id=peer, device_id_type=MESH)

    @pl.when(core == 0)
    def _():
        greet(chip_peer)
        greet({"grp": 1, "slab": beyond})
        greet({"grp": 3, "slab": beyond})

    @pl.when(core == 1)
    def _():
        greet(core_peer)
        greet(cross_peer)
        greet({"grp": 1, "slab": beyond})
        greet({"grp": 3, "slab": beyond})

    occ_copy.wait()
    weights = [
        occ_ref[s].astype(jnp.float32) * (valence_norm / (OCC_DEN * s_dev * 4))
        for s in range(s_dev)
    ]

    def density_part(h, i):
        load(h, i).wait()

        def tile_step(t, carry):
            lanes = pl.ds(pl.multiple_of(i * width + t * STEP, STEP), STEP)
            total = jnp.zeros((half, STEP), jnp.float32)
            for s in range(s_dev):
                wide = held_ref[s, h * half : (h + 1) * half, lanes].astype(jnp.float32)
                total = total + (wide * weights[s]) * wide
            part[h, :, lanes] = total
            return carry

        lax.fori_loop(0, width // STEP, tile_step, 0)

    for i in range(CHUNKS):
        density_part(1, i)

    @pl.when(core == 0)
    def _():
        pl.semaphore_wait(barrier, 3)
        pl.semaphore_signal(group_sem, inc=1, device_id=core_peer, device_id_type=MESH)
        for i in range(CHUNKS):
            to_core(i).start()

    for i in range(CHUNKS):
        density_part(0, i)
        if i == CHUNKS - 2:

            @pl.when(core == 1)
            def _():
                pl.semaphore_wait(group_sem, 1)
                for j in range(CHUNKS - 1):
                    to_core(j).start()

    @pl.when(core == 1)
    def _():
        to_core(CHUNKS - 1).start()

    core_copy.wait()
    first_rows = lax.broadcasted_iota(jnp.int32, (8, LANES), 0) < 4
    with_core = (1 - chip).astype(jnp.float32)
    is_low = core == 0

    for i in range(CHUNKS):
        to_core(i).wait_recv()
        chip_sum[:, cols(i)] = (part[core, :, cols(i)] + from_core[:, cols(i)]) + with_core * core_half[:, cols(i)]
        to_chip(i).start()

    edge_rows = pl.ds(pl.multiple_of(core * 8, 8), 8)
    for t in range(n_tiles // 2):
        front = chip_sum[edge_rows, t * LANES : (t + 1) * LANES]
        back = chip_sum[edge_rows, cells // 2 + t * LANES : cells // 2 + (t + 1) * LANES]
        front_turned, back_turned = pltpu.roll(front, 4, 0), pltpu.roll(back, 4, 0)
        low_edge = jnp.where(first_rows, front, back_turned)
        high_edge = jnp.where(first_rows, front_turned, back)
        edge_out[:, t * LANES : (t + 1) * LANES] = jnp.where(is_low, low_edge, high_edge)

    @pl.when(core == 1)
    def _():
        pl.semaphore_wait(barrier, 4)
        pl.semaphore_signal(slab_sem, inc=1, device_id=core_peer, device_id_type=MESH)

    @pl.when(core == 0)
    def _():
        pl.semaphore_wait(slab_sem, 1)

    for k in range(2):
        to_edge(k).start()

    for i in range(CHUNKS):
        to_chip(i).wait_recv()
        dens[:, cols(i)] = chip_sum[:, cols(i)] + from_chip[:, cols(i)]
        to_inner(i).start()

    for k in range(2):
        from_edge(k).wait_recv()
    for t in range(n_tiles // 2):
        lanes = slice(t * LANES, (t + 1) * LANES)
        both = edge_in[0, :, lanes] + edge_in[1, :, lanes]
        turned = pltpu.roll(both, 4, 0)
        outer[:, t * LANES : (t + 1) * LANES] = jnp.where(first_rows, both, turned)
        outer[:, cells // 2 + t * LANES : cells // 2 + (t + 1) * LANES] = jnp.where(first_rows, turned, both)
    for i in range(CHUNKS):
        to_inner(i).wait_recv()

    lane = lax.broadcasted_iota(jnp.int32, (1, LANES), 1)
    inner = lane % NY
    low = lane < NY
    inner_rows = jnp.where(is_low, first_rows.astype(jnp.int32), 1 - first_rows.astype(jnp.int32)) == 1

    def field(t):
        lanes = pl.ds(pl.multiple_of((t % n_tiles) * LANES, LANES), LANES)
        edge = jnp.where(inner_rows, inner_in[:, lanes], outer[:, lanes])
        return jnp.concatenate([dens[:, lanes], edge], axis=0)

    def flow_step(t, carry):
        centre = field(t)
        left = field(t + n_tiles - 1)
        right = field(t + 1)
        swapped = swap_halves(centre)
        grad_x = along_x(left, swap_halves(left), swapped, right, swap_halves(right), low)
        grad_y = along_y(centre, swapped, inner)
        grad_z = along_z(centre)
        sigma = grad_x * grad_x + grad_y * grad_y + grad_z * grad_z
        root = jnp.exp2(jnp.log2(centre) * (-1.0 / 3.0))
        root2 = root * root
        root4 = root2 * root2
        share = 1.0 / (1.0 + u_scale * (sigma * (root4 * root4)))
        flow = flow_scale * (root4 * (share * share))
        d_dens = (slope_scale * (centre * root2)) * (
            (1.0 + kappa) + share * (2.0 * kappa * share - 3.0 * kappa)
        )
        flow_y = flow * grad_y
        div_y = along_y(flow_y[:half], swap_halves(flow_y[:half]), inner)
        div_z = along_z(flow * grad_z)[:half]
        lanes = pl.ds(pl.multiple_of((t % n_tiles) * LANES, LANES), LANES)
        flow_x[:, lanes] = (flow * grad_x)[:half]
        local[:, lanes] = d_dens[:half] - (div_y + div_z)
        return carry

    def pot_step(t, carry):
        def at(k):
            return flow_x[:, pl.ds(pl.multiple_of((k % n_tiles) * LANES, LANES), LANES)]

        lanes = pl.ds(pl.multiple_of((t % n_tiles) * LANES, LANES), LANES)
        left, centre, right = at(t + n_tiles - 1), at(t), at(t + 1)
        div_x = along_x(
            left, swap_halves(left), swap_halves(centre), right, swap_halves(right), low
        )
        pot_ref[own_rows(), lanes] = local[:, lanes] - div_x
        return carry

    lax.fori_loop(0, n_tiles, flow_step, 0, unroll=8)
    tiles = width // LANES
    for i in range(CHUNKS):
        lax.fori_loop(i * tiles, (i + 1) * tiles, pot_step, 0, unroll=True)
        to_pot(i).start()
    for i in range(CHUNKS):
        to_core(i).wait_send()
        to_chip(i).wait_send()
        to_inner(i).wait_send()
        to_pot(i).wait()
    for k in range(2):
        to_edge(k).wait_send()


def apply_kernel(held_ref, pot_ref, applied_ref, out_ref, staged, store_sem, pot_sem):
    s_dev, planes, cells = held_ref.shape
    width = cells // STORES
    pot_copy = pltpu.make_async_copy(pot_ref, out_ref, pot_sem)
    pot_copy.start()

    def store(i):
        cols = pl.ds(i * width, width)
        return pltpu.make_async_copy(staged.at[:, :, cols], applied_ref.at[:, :, cols], store_sem.at[i])

    for i in range(STORES):
        cols = pl.ds(i * width, width)
        pot = pot_ref[:, cols].astype(jnp.bfloat16)

        def state_step(s, carry):
            staged[s, :, cols] = held_ref[s, :, cols] * pot
            return carry

        lax.fori_loop(0, s_dev, state_step, 0, unroll=8)
        store(i).start()
    for i in range(STORES):
        store(i).wait()
    pot_copy.wait()


def body(slabs, states, core_density, occupancy):
    s_dev, planes, cells = states.shape
    half = planes // 2
    vmem = pl.BlockSpec(memory_space=pltpu.VMEM)
    hbm = pl.BlockSpec(memory_space=pltpu.HBM)
    states = pltpu.with_memory_space_constraint(states, pltpu.HBM)
    core_density = pltpu.with_memory_space_constraint(core_density, pltpu.HBM)
    occupancy = pltpu.with_memory_space_constraint(occupancy, pltpu.HBM)

    def rows(count):
        return pltpu.VMEM((count, cells), jnp.float32)

    def sems(count):
        return pltpu.SemaphoreType.DMA((count,))

    held, pot = pl.pallas_call(
        functools.partial(potential_kernel, slabs),
        out_shape=(
            pltpu.VMEM((s_dev, planes, cells), jnp.bfloat16),
            pltpu.VMEM((planes, cells), jnp.float32),
        ),
        in_specs=[hbm, hbm, hbm],
        out_specs=(vmem, vmem),
        scratch_shapes=[
            pltpu.SMEM((s_dev,), jnp.int32),
            pltpu.VMEM((2, half, cells), jnp.float32),
            rows(half),
            rows(half),
            rows(half),
            rows(half),
            rows(half),
            rows(8),
            pltpu.VMEM((8, cells // 2), jnp.float32),
            pltpu.VMEM((2, 8, cells // 2), jnp.float32),
            rows(8),
            rows(half),
            rows(half),
            sems(2 * CHUNKS),
            sems(2),
            pltpu.SemaphoreType.REGULAR,
            pltpu.SemaphoreType.REGULAR,
        ]
        + [sems(CHUNKS)] * 6
        + [sems(2)] * 2
        + [sems(CHUNKS)] * 2,
        compiler_params=pltpu.CompilerParams(
            collective_id=0, has_side_effects=True, vmem_limit_bytes=24 * 1024 * 1024
        ),
        name="potential",
    )(occupancy, states, core_density)
    return pl.pallas_call(
        apply_kernel,
        out_shape=(
            jax.ShapeDtypeStruct((s_dev, planes, cells), jnp.bfloat16),
            jax.ShapeDtypeStruct((planes, cells), jnp.float32),
        ),
        in_specs=[vmem, vmem],
        out_specs=(hbm, hbm),
        scratch_shapes=[
            pltpu.VMEM((s_dev, planes, cells), jnp.bfloat16),
            sems(STORES),
            pltpu.SemaphoreType.DMA,
        ],
        compiler_params=pltpu.CompilerParams(vmem_limit_bytes=32 * 1024 * 1024),
        name="apply",
    )(held, pot)


def solution(mesh):
    placed = (P("grp", "slab", None), P("slab", None), P("grp"))
    return jax.shard_map(
        functools.partial(body, mesh.shape["slab"]),
        mesh=mesh,
        in_specs=placed,
        out_specs=(P("grp", "slab", None), P("slab", None)),
        check_vma=False,
    )
```

time: 30.7 us -> 29 us (0.945)
  Pallas kernels: 29.2 us -> 28.3 us
  local copies, waits for them, and re-layouts: 0.65 us -> 0 us
    pallas_call x1, Pallas kernels: 25.7 us -> 24.7 us  [body(): pl.pallas_call(functools.partial(potential_kernel, slabs), out_shape=(plt...]
    unnamed x2 -> x0, local copies, waits for them, and re-layouts: 0.65 us -> none
where the time goes in v3:
time: 29 us; the launch traced here: 28.9 us
  Pallas kernels  28.3 us (98%)
  between operations  0.64 us (2%)
    pallas_call x1, Pallas kernels, body(): pl.pallas_call(functools.partial(potential_kernel, slabs), out_shape=(plt...  24.7 us
    pallas_call x1, Pallas kernels, body(): pl.pallas_call(apply_kernel, out_shape=(jax.ShapeDtypeStruct((s_dev, plan...  3.55 us

profile of v3, /device:TPU:1, one launch (start us, length us, event | category | flops | bytes accessed | tf_op | source)
XLA Modules:
  0.0 28.9 jit_solution(5500540134068634756)
XLA Ops:
  0.6 24.7 %potential.1 = (bf16[32,32,4096]{2,1,0:T(8,128)(2,1)S(1)}, f32[32,4096]{1,0:T(8,128)S(1)}) custom-call(s32[32]{0:T(128)} %occ_hbm.1, bf16[32,32,4096]{2,1,0:T(8,128)(2,1)} %states_ref.1, f32[32,4096]{1,0:T(8,128)} %core_ref.1), custom_call_target="tpu_custom_call" | custom-call | tf_op jit(solution)/shard_map/potential/pallas_call | solution.py:377
  25.3 3.6 %apply.1 = (bf16[32,32,4096]{2,1,0:T(8,128)(2,1)}, f32[32,4096]{1,0:T(8,128)}) custom-call(bf16[32,32,4096]{2,1,0:T(8,128)(2,1)S(1)} %get-tuple-element.4.held_ref, f32[32,4096]{1,0:T(8,128)S(1)} %get-tuple-element.5.pot_ref), custom_call_target="tpu_custom_call" | custom-call | tf_op jit(solution)/shard_map/apply/pallas_call | solution.py:412

commit v4 on v3

--- a/solution.py
+++ b/solution.py
@@ -107,11 +107,12 @@
     grp = lax.axis_index("grp")
     slab = lax.axis_index("slab")
     chip = grp // 2
-    core = grp % 2
-    core_peer = {"grp": chip * 2 + 1 - core, "slab": slab}
-    chip_peer = {"grp": (1 - chip) * 2 + core, "slab": slab}
-    cross_peer = {"grp": (1 - chip) * 2 + 1 - core, "slab": slab}
-    beyond = (slab + slabs - 1 + 2 * core) % slabs
+    upper = 1 - grp % 2
+    core_peer = {"grp": chip * 2 + upper, "slab": slab}
+    chip_peer = {"grp": (1 - chip) * 2 + 1 - upper, "slab": slab}
+    cross_peer = {"grp": (1 - chip) * 2 + upper, "slab": slab}
+    beyond = (slab + slabs - 1 + 2 * upper) % slabs
+    wrapped = slab % 8 == 0
     edge_chips = (chip, 1 - chip)
 
     def cols(i):
@@ -128,7 +129,7 @@
 
     def to_core(i):
         return remote(
-            part.at[1 - core, :, cols(i)], from_core.at[:, cols(i)], core_send.at[i], core_recv.at[i], core_peer
+            part.at[1 - upper, :, cols(i)], from_core.at[:, cols(i)], core_send.at[i], core_recv.at[i], core_peer
         )
 
     def to_chip(i):
@@ -137,20 +138,20 @@
         )
 
     def to_edge(k):
-        peer = {"grp": edge_chips[k] * 2 + 1 - core, "slab": beyond}
+        peer = {"grp": edge_chips[k] * 2 + upper, "slab": beyond}
         return remote(edge_out, edge_in.at[chip], edge_send.at[k], edge_recv.at[chip], peer)
 
     def from_edge(k):
         return remote(edge_out, edge_in.at[k], edge_send.at[k], edge_recv.at[k], core_peer)
 
     def to_inner(i):
-        rows = pl.ds(pl.multiple_of((1 - core) * 8, 8), 8)
+        rows = pl.ds(pl.multiple_of((1 - upper) * 8, 8), 8)
         return remote(
             dens.at[rows, cols(i)], inner_in.at[:, cols(i)], inner_send.at[i], inner_recv.at[i], core_peer
         )
 
     def own_rows():
-        return pl.ds(pl.multiple_of(core * half, half), half)
+        return pl.ds(pl.multiple_of(upper * half, half), half)
 
     def to_pot(i):
         where = pot_ref.at[own_rows(), cols(i)]
@@ -169,18 +170,18 @@
     def greet(peer):
         pl.semaphore_signal(barrier, inc=1, device_id=peer, device_id_type=MESH)
 
-    @pl.when(core == 0)
+    @pl.when(upper == 0)
     def _():
         greet(chip_peer)
-        greet({"grp": 1, "slab": beyond})
-        greet({"grp": 3, "slab": beyond})
-
-    @pl.when(core == 1)
+        greet({"grp": 0, "slab": beyond})
+        greet({"grp": 2, "slab": beyond})
+
+    @pl.when(upper == 1)
     def _():
         greet(core_peer)
         greet(cross_peer)
-        greet({"grp": 1, "slab": beyond})
-        greet({"grp": 3, "slab": beyond})
+        greet({"grp": 0, "slab": beyond})
+        greet({"grp": 2, "slab": beyond})
 
     occ_copy.wait()
     weights = [
@@ -202,60 +203,95 @@
 
         lax.fori_loop(0, width // STEP, tile_step, 0)
 
+    first_rows = lax.broadcasted_iota(jnp.int32, (8, LANES), 0) < 4
+    with_core = (1 - chip).astype(jnp.float32)
+    is_low = upper == 0
+
+    def sum_chip():
+        core_copy.wait()
+        for i in range(CHUNKS):
+            to_core(i).wait_recv()
+            chip_sum[:, cols(i)] = (part[upper, :, cols(i)] + from_core[:, cols(i)]) + with_core * core_half[:, cols(i)]
+
+        edge_rows = pl.ds(pl.multiple_of(upper * 8, 8), 8)
+
+        def pack(t, carry):
+            lanes = pl.ds(pl.multiple_of(t * LANES, LANES), LANES)
+            front = chip_sum[edge_rows, lanes]
+            back = chip_sum[edge_rows, pl.ds(pl.multiple_of(cells // 2 + t * LANES, LANES), LANES)]
+            front_turned, back_turned = pltpu.roll(front, 4, 0), pltpu.roll(back, 4, 0)
+            low_edge = jnp.where(first_rows, front, back_turned)
+            high_edge = jnp.where(first_rows, front_turned, back)
+            edge_out[:, lanes] = jnp.where(is_low, low_edge, high_edge)
+            return carry
+
+        lax.fori_loop(0, n_tiles // 2, pack, 0, unroll=4)
+
+    def send_chip():
+        for i in range(CHUNKS):
+            to_chip(i).start()
+
+    def send_edges():
+        for k in range(2):
+            to_edge(k).start()
+
+    def meet_slabs():
+        pl.semaphore_wait(barrier, 4)
+        pl.semaphore_signal(slab_sem, inc=1, device_id=core_peer, device_id_type=MESH)
+
     for i in range(CHUNKS):
         density_part(1, i)
 
-    @pl.when(core == 0)
+    @pl.when(upper == 0)
     def _():
         pl.semaphore_wait(barrier, 3)
         pl.semaphore_signal(group_sem, inc=1, device_id=core_peer, device_id_type=MESH)
         for i in range(CHUNKS):
             to_core(i).start()
 
-    for i in range(CHUNKS):
+    for i in range(CHUNKS - 1):
         density_part(0, i)
-        if i == CHUNKS - 2:
-
-            @pl.when(core == 1)
-            def _():
-                pl.semaphore_wait(group_sem, 1)
-                for j in range(CHUNKS - 1):
-                    to_core(j).start()
-
-    @pl.when(core == 1)
+
+    @pl.when(upper == 1)
+    def _():
+        pl.semaphore_wait(group_sem, 1)
+        for i in range(CHUNKS - 1):
+            to_core(i).start()
+        sum_chip()
+
+        @pl.when(jnp.logical_not(wrapped))
+        def _():
+            meet_slabs()
+            send_edges()
+
+        send_chip()
+
+    density_part(0, CHUNKS - 1)
+
+    @pl.when(upper == 1)
     def _():
         to_core(CHUNKS - 1).start()
 
-    core_copy.wait()
-    first_rows = lax.broadcasted_iota(jnp.int32, (8, LANES), 0) < 4
-    with_core = (1 - chip).astype(jnp.float32)
-    is_low = core == 0
-
-    for i in range(CHUNKS):
-        to_core(i).wait_recv()
-        chip_sum[:, cols(i)] = (part[core, :, cols(i)] + from_core[:, cols(i)]) + with_core * core_half[:, cols(i)]
-        to_chip(i).start()
-
-    edge_rows = pl.ds(pl.multiple_of(core * 8, 8), 8)
-    for t in range(n_tiles // 2):
-        front = chip_sum[edge_rows, t * LANES : (t + 1) * LANES]
-        back = chip_sum[edge_rows, cells // 2 + t * LANES : cells // 2 + (t + 1) * LANES]
-        front_turned, back_turned = pltpu.roll(front, 4, 0), pltpu.roll(back, 4, 0)
-        low_edge = jnp.where(first_rows, front, back_turned)
-        high_edge = jnp.where(first_rows, front_turned, back)
-        edge_out[:, t * LANES : (t + 1) * LANES] = jnp.where(is_low, low_edge, high_edge)
-
-    @pl.when(core == 1)
-    def _():
-        pl.semaphore_wait(barrier, 4)
-        pl.semaphore_signal(slab_sem, inc=1, device_id=core_peer, device_id_type=MESH)
-
-    @pl.when(core == 0)
+    @pl.when(upper == 0)
+    def _():
+        sum_chip()
+
+        @pl.when(jnp.logical_not(wrapped))
+        def _():
+            pl.semaphore_wait(slab_sem, 1)
+            send_edges()
+
+        send_chip()
+
+    @pl.when(wrapped & (upper == 1))
+    def _():
+        meet_slabs()
+        send_edges()
+
+    @pl.when(wrapped & (upper == 0))
     def _():
         pl.semaphore_wait(slab_sem, 1)
-
-    for k in range(2):
-        to_edge(k).start()
+        send_edges()
 
     for i in range(CHUNKS):
         to_chip(i).wait_recv()

time: 29 us -> 24.9 us (0.86)
  Pallas kernels: 28.3 us -> 24.1 us
    pallas_call x1, Pallas kernels: 24.7 us -> 20.6 us  [body(): pl.pallas_call(functools.partial(potential_kernel, slabs), out_shape=(plt...]
where the time goes in v4:
time: 24.9 us; the launch traced here: 24.8 us
  Pallas kernels  24.1 us (97%)
  between operations  0.64 us (3%)
    pallas_call x1, Pallas kernels, body(): pl.pallas_call(functools.partial(potential_kernel, slabs), out_shape=(plt...  20.6 us
    pallas_call x1, Pallas kernels, body(): pl.pallas_call(apply_kernel, out_shape=(jax.ShapeDtypeStruct((s_dev, plan...  3.55 us

profile of v4, /device:TPU:1, one launch (start us, length us, event | category | flops | bytes accessed | tf_op | source)
XLA Modules:
  0.0 24.8 jit_solution(426666113390740461)
XLA Ops:
  0.6 20.6 %potential.1 = (bf16[32,32,4096]{2,1,0:T(8,128)(2,1)S(1)}, f32[32,4096]{1,0:T(8,128)S(1)}) custom-call(s32[32]{0:T(128)} %occ_hbm.1, bf16[32,32,4096]{2,1,0:T(8,128)(2,1)} %states_ref.1, f32[32,4096]{1,0:T(8,128)} %core_ref.1), custom_call_target="tpu_custom_call" | custom-call | tf_op jit(solution)/shard_map/potential/pallas_call | solution.py:413
  21.2 3.6 %apply.1 = (bf16[32,32,4096]{2,1,0:T(8,128)(2,1)}, f32[32,4096]{1,0:T(8,128)}) custom-call(bf16[32,32,4096]{2,1,0:T(8,128)(2,1)S(1)} %get-tuple-element.4.held_ref, f32[32,4096]{1,0:T(8,128)S(1)} %get-tuple-element.5.pot_ref), custom_call_target="tpu_custom_call" | custom-call | tf_op jit(solution)/shard_map/apply/pallas_call | solution.py:448

commit v5 on v4

--- a/solution.py
+++ b/solution.py
@@ -29,6 +29,9 @@
 
 CHUNKS = 4
 STEP = 4 * LANES
+SPAN = 32
+FAR_SPAN = 32
+NEAR_SPAN = 16
 STORES = 8
 
 
@@ -84,6 +87,8 @@
     outer,
     flow_x,
     local,
+    near_rest,
+    near_z,
     load_sem,
     misc_sem,
     group_sem,
@@ -144,18 +149,29 @@
     def from_edge(k):
         return remote(edge_out, edge_in.at[k], edge_send.at[k], edge_recv.at[k], core_peer)
 
+    def shifted(i):
+        return pl.ds(pl.multiple_of(i * width + LANES, LANES), width)
+
     def to_inner(i):
         rows = pl.ds(pl.multiple_of((1 - upper) * 8, 8), 8)
         return remote(
-            dens.at[rows, cols(i)], inner_in.at[:, cols(i)], inner_send.at[i], inner_recv.at[i], core_peer
+            dens.at[rows, shifted(i)], inner_in.at[:, shifted(i)], inner_send.at[i], inner_recv.at[i], core_peer
         )
 
     def own_rows():
         return pl.ds(pl.multiple_of(upper * half, half), half)
 
+    near_out = pl.ds(pl.multiple_of(upper * 24, 8), 8)
+    far_out = pl.ds(pl.multiple_of(8 + upper * 8, 8), 8)
+
     def to_pot(i):
-        where = pot_ref.at[own_rows(), cols(i)]
+        span = NEAR_SPAN * LANES
+        where = pot_ref.at[near_out, pl.ds(pl.multiple_of(i * span, LANES), span)]
         return remote(where, where, pot_send.at[i], pot_recv.at[i], core_peer)
+
+    def to_pot_far():
+        where = pot_ref.at[far_out, :]
+        return remote(where, where, pot_send.at[CHUNKS], pot_recv.at[CHUNKS], core_peer)
 
     occ_copy = pltpu.make_async_copy(occ_hbm, occ_ref, misc_sem.at[0])
     occ_copy.start()
@@ -293,39 +309,33 @@
         pl.semaphore_wait(slab_sem, 1)
         send_edges()
 
-    for i in range(CHUNKS):
-        to_chip(i).wait_recv()
-        dens[:, cols(i)] = chip_sum[:, cols(i)] + from_chip[:, cols(i)]
-        to_inner(i).start()
-
-    for k in range(2):
-        from_edge(k).wait_recv()
-    for t in range(n_tiles // 2):
-        lanes = slice(t * LANES, (t + 1) * LANES)
-        both = edge_in[0, :, lanes] + edge_in[1, :, lanes]
-        turned = pltpu.roll(both, 4, 0)
-        outer[:, t * LANES : (t + 1) * LANES] = jnp.where(first_rows, both, turned)
-        outer[:, cells // 2 + t * LANES : cells // 2 + (t + 1) * LANES] = jnp.where(first_rows, turned, both)
-    for i in range(CHUNKS):
-        to_inner(i).wait_recv()
-
     lane = lax.broadcasted_iota(jnp.int32, (1, LANES), 1)
     inner = lane % NY
     low = lane < NY
-    inner_rows = jnp.where(is_low, first_rows.astype(jnp.int32), 1 - first_rows.astype(jnp.int32)) == 1
-
-    def field(t):
-        lanes = pl.ds(pl.multiple_of((t % n_tiles) * LANES, LANES), LANES)
-        edge = jnp.where(inner_rows, inner_in[:, lanes], outer[:, lanes])
-        return jnp.concatenate([dens[:, lanes], edge], axis=0)
-
-    def flow_step(t, carry):
-        centre = field(t)
-        left = field(t + n_tiles - 1)
-        right = field(t + 1)
-        swapped = swap_halves(centre)
-        grad_x = along_x(left, swap_halves(left), swapped, right, swap_halves(right), low)
-        grad_y = along_y(centre, swapped, inner)
+    row = lax.broadcasted_iota(jnp.int32, (8, LANES), 0)
+    own_four = jnp.where(is_low, row, 7 - row) < 4
+    own_two = jnp.where(is_low, row, 7 - row) < 2
+    near = pl.ds(pl.multiple_of(upper * 8, 8), 8)
+    far = pl.ds(pl.multiple_of((1 - upper) * 8, 8), 8)
+
+    tiles = width // LANES
+    reach = (tiles + 2) * LANES
+    last = n_tiles * LANES
+    first_copy, last_copy = slice(last + LANES, last + 2 * LANES), slice(0, LANES)
+    first_tile, last_tile = slice(LANES, 2 * LANES), slice(last, last + LANES)
+
+    def at(j):
+        return slice(j * LANES, (j + 1) * LANES)
+
+    def total(i):
+        to_chip(i).wait_recv()
+        dens[:, shifted(i)] = chip_sum[:, cols(i)] + from_chip[:, cols(i)]
+        to_inner(i).start()
+
+    def flows(fields, turned, j):
+        centre = fields[j]
+        grad_x = along_x(fields[j - 1], turned[j - 1], turned[j], fields[j + 1], turned[j + 1], low)
+        grad_y = along_y(centre, turned[j], inner)
         grad_z = along_z(centre)
         sigma = grad_x * grad_x + grad_y * grad_y + grad_z * grad_z
         root = jnp.exp2(jnp.log2(centre) * (-1.0 / 3.0))
@@ -336,36 +346,113 @@
         d_dens = (slope_scale * (centre * root2)) * (
             (1.0 + kappa) + share * (2.0 * kappa * share - 3.0 * kappa)
         )
-        flow_y = flow * grad_y
-        div_y = along_y(flow_y[:half], swap_halves(flow_y[:half]), inner)
-        div_z = along_z(flow * grad_z)[:half]
-        lanes = pl.ds(pl.multiple_of((t % n_tiles) * LANES, LANES), LANES)
-        flow_x[:, lanes] = (flow * grad_x)[:half]
-        local[:, lanes] = d_dens[:half] - (div_y + div_z)
+        return flow * grad_x, flow * grad_y, flow * grad_z, d_dens
+
+    def first_pass(where, count):
+        window = [ref.at[:, where] for ref in (dens, inner_in, flow_x, local, near_rest, near_z)]
+        dens_w, inner_w, flow_w, local_w, rest_w, z_w = window
+        fields = [jnp.concatenate([dens_w[:, at(j)], inner_w[:, at(j)]], axis=0) for j in range(count + 2)]
+        turned = [swap_halves(f) for f in fields]
+        for j in range(1, count + 1):
+            part_x, part_y, part_z, d_dens = flows(fields, turned, j)
+            part_y = part_y[:half]
+            rest = d_dens[:half] - along_y(part_y, swap_halves(part_y), inner)
+            flow_w[:, at(j)] = part_x[:half]
+            local_w[:, at(j)] = rest - along_z(part_z)[:half]
+            rest_w[:, at(j)] = jnp.where(is_low, rest[:8], rest[8:])
+            z_w[:, at(j)] = jnp.where(is_low, part_z[:8], part_z[8:half])
+
+    def second_pass(g, carry):
+        where = pl.ds(pl.multiple_of(g * SPAN * LANES, LANES), (SPAN + 2) * LANES)
+        dens_w, flow_w, local_w = (ref.at[near, where] for ref in (dens, flow_x, local))
+        outer_w, rest_w, z_w = (ref.at[:, where] for ref in (outer, near_rest, near_z))
+        fields = [
+            jnp.where(own_four, outer_w[:, at(j)], pltpu.roll(dens_w[:, at(j)], 4, 0)) for j in range(SPAN + 2)
+        ]
+        turned = [swap_halves(f) for f in fields]
+        for j in range(1, SPAN + 1):
+            part_x, part_y, part_z, d_dens = flows(fields, turned, j)
+            rest = d_dens - along_y(part_y, swap_halves(part_y), inner)
+            rest = jnp.where(own_two, pltpu.roll(rest, 4, 0), rest_w[:, at(j)])
+            old_z = z_w[:, at(j)]
+            row_z = jnp.where(
+                first_rows,
+                pltpu.roll(jnp.where(is_low, part_z, old_z), 6, 0),
+                pltpu.roll(jnp.where(is_low, old_z, part_z), 2, 0),
+            )
+            div_z = along_z(row_z)
+            div_z = jnp.where(is_low, pltpu.roll(div_z, 6, 0), pltpu.roll(div_z, 2, 0))
+            local_w[:, at(j)] = jnp.where(own_four, rest - div_z, local_w[:, at(j)])
+            flow_w[:, at(j)] = jnp.where(own_two, pltpu.roll(part_x, 4, 0), flow_w[:, at(j)])
         return carry
 
-    def pot_step(t, carry):
-        def at(k):
-            return flow_x[:, pl.ds(pl.multiple_of((k % n_tiles) * LANES, LANES), LANES)]
-
-        lanes = pl.ds(pl.multiple_of((t % n_tiles) * LANES, LANES), LANES)
-        left, centre, right = at(t + n_tiles - 1), at(t), at(t + 1)
-        div_x = along_x(
-            left, swap_halves(left), swap_halves(centre), right, swap_halves(right), low
-        )
-        pot_ref[own_rows(), lanes] = local[:, lanes] - div_x
+    def finish(rows, out_rows, g, span):
+        where = pl.ds(pl.multiple_of(g * span * LANES, LANES), (span + 2) * LANES)
+        flow_w, local_w = flow_x.at[rows, where], local.at[rows, where]
+        out_w = pot_ref.at[out_rows, pl.ds(pl.multiple_of(g * span * LANES, LANES), span * LANES)]
+        fields = [flow_w[:, at(j)] for j in range(span + 2)]
+        turned = [swap_halves(f) for f in fields]
+        for j in range(1, span + 1):
+            div_x = along_x(fields[j - 1], turned[j - 1], turned[j], fields[j + 1], turned[j + 1], low)
+            out_w[:, at(j - 1)] = local_w[:, at(j)] - div_x
+
+    def finish_far(g, carry):
+        finish(far, far_out, g, FAR_SPAN)
         return carry
 
-    lax.fori_loop(0, n_tiles, flow_step, 0, unroll=8)
-    tiles = width // LANES
-    for i in range(CHUNKS):
-        lax.fori_loop(i * tiles, (i + 1) * tiles, pot_step, 0, unroll=True)
-        to_pot(i).start()
+    def finish_near(g, carry):
+        finish(near, near_out, g, NEAR_SPAN)
+        to_pot(g).start()
+        return carry
+
+    def wrap(ref, rows):
+        ref[rows, first_copy] = ref[rows, first_tile]
+        ref[rows, last_copy] = ref[rows, last_tile]
+
+    everything = slice(None)
+    total(0)
+    dens[:, first_copy] = dens[:, first_tile]
+    total(1)
+    to_inner(0).wait_recv()
+    inner_in[:, first_copy] = inner_in[:, first_tile]
+    first_pass(pl.ds(LANES, tiles * LANES), tiles - 2)
+
+    def follow(i, carry):
+        @pl.when(i < CHUNKS)
+        def _():
+            total(i)
+
+        to_inner(i - 1).wait_recv()
+        first_pass(pl.ds(pl.multiple_of((i - 1) * width - LANES, LANES), reach), tiles)
+        return carry
+
+    lax.fori_loop(2, CHUNKS + 1, follow, 0)
+    dens[:, last_copy] = dens[:, last_tile]
+    inner_in[:, last_copy] = inner_in[:, last_tile]
+    first_pass(pl.ds(last - LANES, 3 * LANES), 1)
+    first_pass(pl.ds(0, 3 * LANES), 1)
+    wrap(flow_x, everything)
+    lax.fori_loop(0, n_tiles // FAR_SPAN, finish_far, 0)
+    to_pot_far().start()
+    for k in range(2):
+        from_edge(k).wait_recv()
+
+    for t in range(n_tiles // 2):
+        both = edge_in[0, :, at(t)] + edge_in[1, :, at(t)]
+        turned = pltpu.roll(both, 4, 0)
+        outer[:, at(t + 1)] = jnp.where(first_rows, both, turned)
+        outer[:, at(t + 1 + n_tiles // 2)] = jnp.where(first_rows, turned, both)
+    wrap(outer, everything)
+    lax.fori_loop(0, n_tiles // SPAN, second_pass, 0)
+    wrap(flow_x, near)
+    lax.fori_loop(0, n_tiles // NEAR_SPAN, finish_near, 0)
     for i in range(CHUNKS):
         to_core(i).wait_send()
         to_chip(i).wait_send()
         to_inner(i).wait_send()
+    for i in range(n_tiles // NEAR_SPAN):
         to_pot(i).wait()
+    to_pot_far().wait()
     for k in range(2):
         to_edge(k).wait_send()
 
@@ -406,6 +493,9 @@
 
     def rows(count):
         return pltpu.VMEM((count, cells), jnp.float32)
+
+    def wide(count):
+        return pltpu.VMEM((count, cells + 2 * LANES), jnp.float32)
 
     def sems(count):
         return pltpu.SemaphoreType.DMA((count,))
@@ -425,13 +515,15 @@
             rows(half),
             rows(half),
             rows(half),
-            rows(half),
-            rows(8),
+            wide(half),
+            wide(8),
             pltpu.VMEM((8, cells // 2), jnp.float32),
             pltpu.VMEM((2, 8, cells // 2), jnp.float32),
-            rows(8),
-            rows(half),
-            rows(half),
+            wide(8),
+            wide(half),
+            wide(half),
+            wide(8),
+            wide(8),
             sems(2 * CHUNKS),
             sems(2),
             pltpu.SemaphoreType.REGULAR,
@@ -439,7 +531,7 @@
         ]
         + [sems(CHUNKS)] * 6
         + [sems(2)] * 2
-        + [sems(CHUNKS)] * 2,
+        + [sems(CHUNKS + 1)] * 2,
         compiler_params=pltpu.CompilerParams(
             collective_id=0, has_side_effects=True, vmem_limit_bytes=24 * 1024 * 1024
         ),

time: 24.9 us -> 23.4 us (0.940)
  Pallas kernels: 24.1 us -> 22.7 us
    pallas_call x1, Pallas kernels: 20.6 us -> 19.1 us  [body(): pl.pallas_call(functools.partial(potential_kernel, slabs), out_shape=(plt...]
where the time goes in v5:
time: 23.4 us; the launch traced here: 23.3 us
  Pallas kernels  22.7 us (97%)
  between operations  0.64 us (3%)
    pallas_call x1, Pallas kernels, body(): pl.pallas_call(functools.partial(potential_kernel, slabs), out_shape=(plt...  19.1 us
    pallas_call x1, Pallas kernels, body(): pl.pallas_call(apply_kernel, out_shape=(jax.ShapeDtypeStruct((s_dev, plan...  3.55 us

profile of v5, /device:TPU:1, one launch (start us, length us, event | category | flops | bytes accessed | tf_op | source)
XLA Modules:
  0.0 23.3 jit_solution(6778568725027172954)
XLA Ops:
  0.6 19.1 %potential.1 = (bf16[32,32,4096]{2,1,0:T(8,128)(2,1)S(1)}, f32[32,4096]{1,0:T(8,128)S(1)}) custom-call(s32[32]{0:T(128)} %occ_hbm.1, bf16[32,32,4096]{2,1,0:T(8,128)(2,1)} %states_ref.1, f32[32,4096]{1,0:T(8,128)} %core_ref.1), custom_call_target="tpu_custom_call" | custom-call | tf_op jit(solution)/shard_map/potential/pallas_call | solution.py:503
  19.7 3.6 %apply.1 = (bf16[32,32,4096]{2,1,0:T(8,128)(2,1)}, f32[32,4096]{1,0:T(8,128)}) custom-call(bf16[32,32,4096]{2,1,0:T(8,128)(2,1)S(1)} %get-tuple-element.4.held_ref, f32[32,4096]{1,0:T(8,128)S(1)} %get-tuple-element.5.pot_ref), custom_call_target="tpu_custom_call" | custom-call | tf_op jit(solution)/shard_map/apply/pallas_call | solution.py:540

commit v6 on v5

--- a/solution.py
+++ b/solution.py
@@ -29,6 +29,7 @@
 
 CHUNKS = 4
 STEP = 4 * LANES
+GATE = 2
 SPAN = 32
 FAR_SPAN = 32
 NEAR_SPAN = 16
@@ -93,15 +94,11 @@
     misc_sem,
     group_sem,
     slab_sem,
-    core_send,
+    sent,
     core_recv,
-    chip_send,
     chip_recv,
-    inner_send,
     inner_recv,
-    edge_send,
     edge_recv,
-    pot_send,
     pot_recv,
 ):
     s_dev, planes, cells = states_ref.shape
@@ -118,6 +115,7 @@
     cross_peer = {"grp": (1 - chip) * 2 + upper, "slab": slab}
     beyond = (slab + slabs - 1 + 2 * upper) % slabs
     wrapped = slab % 8 == 0
+    rushed = (slab % 8 == 7) & (upper == 1)
     edge_chips = (chip, 1 - chip)
 
     def cols(i):
@@ -134,20 +132,25 @@
 
     def to_core(i):
         return remote(
-            part.at[1 - upper, :, cols(i)], from_core.at[:, cols(i)], core_send.at[i], core_recv.at[i], core_peer
+            part.at[1 - upper, :, cols(i)], from_core.at[:, cols(i)], sent.at[1], core_recv.at[i], core_peer
         )
 
     def to_chip(i):
         return remote(
-            chip_sum.at[:, cols(i)], from_chip.at[:, cols(i)], chip_send.at[i], chip_recv.at[i], chip_peer
+            chip_sum.at[:, cols(i)], from_chip.at[:, cols(i)], sent.at[2], chip_recv.at[i], chip_peer
         )
 
-    def to_edge(k):
+    def edge_cols(m):
+        return slice(m * width, (m + 1) * width)
+
+    def to_edge(m, k):
         peer = {"grp": edge_chips[k] * 2 + upper, "slab": beyond}
-        return remote(edge_out, edge_in.at[chip], edge_send.at[k], edge_recv.at[chip], peer)
-
-    def from_edge(k):
-        return remote(edge_out, edge_in.at[k], edge_send.at[k], edge_recv.at[k], core_peer)
+        out = edge_out.at[:, edge_cols(m)]
+        return remote(out, edge_in.at[chip, :, edge_cols(m)], sent.at[0], edge_recv.at[2 * m + chip], peer)
+
+    def from_edge(m, k):
+        out = edge_out.at[:, edge_cols(m)]
+        return remote(out, edge_in.at[k, :, edge_cols(m)], sent.at[0], edge_recv.at[2 * m + k], core_peer)
 
     def shifted(i):
         return pl.ds(pl.multiple_of(i * width + LANES, LANES), width)
@@ -155,7 +158,7 @@
     def to_inner(i):
         rows = pl.ds(pl.multiple_of((1 - upper) * 8, 8), 8)
         return remote(
-            dens.at[rows, shifted(i)], inner_in.at[:, shifted(i)], inner_send.at[i], inner_recv.at[i], core_peer
+            dens.at[rows, shifted(i)], inner_in.at[:, shifted(i)], sent.at[3], inner_recv.at[i], core_peer
         )
 
     def own_rows():
@@ -167,19 +170,11 @@
     def to_pot(i):
         span = NEAR_SPAN * LANES
         where = pot_ref.at[near_out, pl.ds(pl.multiple_of(i * span, LANES), span)]
-        return remote(where, where, pot_send.at[i], pot_recv.at[i], core_peer)
+        return remote(where, where, sent.at[4], pot_recv.at[i], core_peer)
 
     def to_pot_far():
         where = pot_ref.at[far_out, :]
-        return remote(where, where, pot_send.at[CHUNKS], pot_recv.at[CHUNKS], core_peer)
-
-    occ_copy = pltpu.make_async_copy(occ_hbm, occ_ref, misc_sem.at[0])
-    occ_copy.start()
-    for h in (1, 0):
-        for i in range(CHUNKS):
-            load(h, i).start()
-    core_copy = pltpu.make_async_copy(core_ref.at[own_rows(), :], core_half, misc_sem.at[1])
-    core_copy.start()
+        return remote(where, where, sent.at[5], pot_recv.at[CHUNKS], core_peer)
 
     barrier = pltpu.get_barrier_semaphore()
 
@@ -198,6 +193,15 @@
         greet(cross_peer)
         greet({"grp": 0, "slab": beyond})
         greet({"grp": 2, "slab": beyond})
+
+    occ_copy = pltpu.make_async_copy(occ_hbm, occ_ref, misc_sem.at[0])
+    occ_copy.start()
+    for i in range(CHUNKS):
+        load(1, i).start()
+    core_copy = pltpu.make_async_copy(core_ref.at[own_rows(), :], core_half, misc_sem.at[1])
+    core_copy.start()
+    for i in range(CHUNKS):
+        load(0, i).start()
 
     occ_copy.wait()
     weights = [
@@ -223,91 +227,99 @@
     with_core = (1 - chip).astype(jnp.float32)
     is_low = upper == 0
 
-    def sum_chip():
-        core_copy.wait()
-        for i in range(CHUNKS):
-            to_core(i).wait_recv()
-            chip_sum[:, cols(i)] = (part[upper, :, cols(i)] + from_core[:, cols(i)]) + with_core * core_half[:, cols(i)]
-
+    def sum_chip(i):
+        to_core(i).wait_recv()
+        chip_sum[:, cols(i)] = (part[upper, :, cols(i)] + from_core[:, cols(i)]) + with_core * core_half[:, cols(i)]
+
+    def pack(m):
         edge_rows = pl.ds(pl.multiple_of(upper * 8, 8), 8)
-
-        def pack(t, carry):
-            lanes = pl.ds(pl.multiple_of(t * LANES, LANES), LANES)
-            front = chip_sum[edge_rows, lanes]
-            back = chip_sum[edge_rows, pl.ds(pl.multiple_of(cells // 2 + t * LANES, LANES), LANES)]
+        for t in range(width // LANES):
+            here = 2 * m * width + t * LANES
+            front = chip_sum[edge_rows, here : here + LANES]
+            back = chip_sum[edge_rows, here + width : here + width + LANES]
             front_turned, back_turned = pltpu.roll(front, 4, 0), pltpu.roll(back, 4, 0)
             low_edge = jnp.where(first_rows, front, back_turned)
             high_edge = jnp.where(first_rows, front_turned, back)
-            edge_out[:, lanes] = jnp.where(is_low, low_edge, high_edge)
-            return carry
-
-        lax.fori_loop(0, n_tiles // 2, pack, 0, unroll=4)
-
-    def send_chip():
-        for i in range(CHUNKS):
-            to_chip(i).start()
-
-    def send_edges():
+            edge_out[:, m * width + t * LANES : m * width + (t + 1) * LANES] = jnp.where(is_low, low_edge, high_edge)
+
+    def send_edges(m):
         for k in range(2):
-            to_edge(k).start()
+            to_edge(m, k).start()
 
     def meet_slabs():
-        pl.semaphore_wait(barrier, 4)
-        pl.semaphore_signal(slab_sem, inc=1, device_id=core_peer, device_id_type=MESH)
+        @pl.when(upper == 1)
+        def _():
+            pl.semaphore_wait(barrier, 4)
+            pl.semaphore_signal(slab_sem, inc=1, device_id=core_peer, device_id_type=MESH)
+
+        @pl.when(upper == 0)
+        def _():
+            pl.semaphore_wait(slab_sem, 1)
+
+    def sum_and_send(m):
+        for i in (2 * m, 2 * m + 1):
+            sum_chip(i)
+        pack(m)
+
+        @pl.when(jnp.logical_not(wrapped))
+        def _():
+            if m == 0:
+                meet_slabs()
+            send_edges(m)
+
+        @pl.when(jnp.logical_not(rushed))
+        def _():
+            for i in (2 * m, 2 * m + 1):
+                to_chip(i).start()
+
+        if m == 1:
+
+            @pl.when(rushed)
+            def _():
+                for i in range(CHUNKS):
+                    to_chip(i).start()
 
     for i in range(CHUNKS):
         density_part(1, i)
+        if i == GATE:
+
+            @pl.when(upper == 0)
+            def _():
+                pl.semaphore_wait(barrier, 3)
+                pl.semaphore_signal(group_sem, inc=1, device_id=core_peer, device_id_type=MESH)
+                for j in range(GATE):
+                    to_core(j).start()
+
+        if i >= GATE:
+
+            @pl.when(upper == 0)
+            def _():
+                to_core(i).start()
+
+    core_copy.wait()
+    for i in range(CHUNKS):
+        if i % 2 == 0:
+            @pl.when(upper == 1)
+            def _():
+                if i == 0:
+                    pl.semaphore_wait(group_sem, 1)
+                sum_and_send(i // 2)
+        density_part(0, i)
+
+        @pl.when(upper == 1)
+        def _():
+            to_core(i).start()
 
     @pl.when(upper == 0)
     def _():
-        pl.semaphore_wait(barrier, 3)
-        pl.semaphore_signal(group_sem, inc=1, device_id=core_peer, device_id_type=MESH)
-        for i in range(CHUNKS):
-            to_core(i).start()
-
-    for i in range(CHUNKS - 1):
-        density_part(0, i)
-
-    @pl.when(upper == 1)
-    def _():
-        pl.semaphore_wait(group_sem, 1)
-        for i in range(CHUNKS - 1):
-            to_core(i).start()
-        sum_chip()
-
-        @pl.when(jnp.logical_not(wrapped))
-        def _():
-            meet_slabs()
-            send_edges()
-
-        send_chip()
-
-    density_part(0, CHUNKS - 1)
-
-    @pl.when(upper == 1)
-    def _():
-        to_core(CHUNKS - 1).start()
-
-    @pl.when(upper == 0)
-    def _():
-        sum_chip()
-
-        @pl.when(jnp.logical_not(wrapped))
-        def _():
-            pl.semaphore_wait(slab_sem, 1)
-            send_edges()
-
-        send_chip()
-
-    @pl.when(wrapped & (upper == 1))
+        for m in range(2):
+            sum_and_send(m)
+
+    @pl.when(wrapped)
     def _():
         meet_slabs()
-        send_edges()
-
-    @pl.when(wrapped & (upper == 0))
-    def _():
-        pl.semaphore_wait(slab_sem, 1)
-        send_edges()
+        for m in range(2):
+            send_edges(m)
 
     lane = lax.broadcasted_iota(jnp.int32, (1, LANES), 1)
     inner = lane % NY
@@ -348,19 +360,18 @@
         )
         return flow * grad_x, flow * grad_y, flow * grad_z, d_dens
 
-    def first_pass(where, count):
-        window = [ref.at[:, where] for ref in (dens, inner_in, flow_x, local, near_rest, near_z)]
-        dens_w, inner_w, flow_w, local_w, rest_w, z_w = window
-        fields = [jnp.concatenate([dens_w[:, at(j)], inner_w[:, at(j)]], axis=0) for j in range(count + 2)]
+    def first_pass(start, count):
+        where = [at(t % n_tiles + 1) for t in range(start - 1, start + count + 1)]
+        fields = [jnp.concatenate([dens[:, w], inner_in[:, w]], axis=0) for w in where]
         turned = [swap_halves(f) for f in fields]
         for j in range(1, count + 1):
             part_x, part_y, part_z, d_dens = flows(fields, turned, j)
             part_y = part_y[:half]
             rest = d_dens[:half] - along_y(part_y, swap_halves(part_y), inner)
-            flow_w[:, at(j)] = part_x[:half]
-            local_w[:, at(j)] = rest - along_z(part_z)[:half]
-            rest_w[:, at(j)] = jnp.where(is_low, rest[:8], rest[8:])
-            z_w[:, at(j)] = jnp.where(is_low, part_z[:8], part_z[8:half])
+            flow_x[:, where[j]] = part_x[:half]
+            local[:, where[j]] = rest - along_z(part_z)[:half]
+            near_rest[:, where[j]] = jnp.where(is_low, rest[:8], rest[8:])
+            near_z[:, where[j]] = jnp.where(is_low, part_z[:8], part_z[8:half])
 
     def second_pass(g, carry):
         where = pl.ds(pl.multiple_of(g * SPAN * LANES, LANES), (SPAN + 2) * LANES)
@@ -411,50 +422,46 @@
 
     everything = slice(None)
     total(0)
-    dens[:, first_copy] = dens[:, first_tile]
     total(1)
     to_inner(0).wait_recv()
-    inner_in[:, first_copy] = inner_in[:, first_tile]
-    first_pass(pl.ds(LANES, tiles * LANES), tiles - 2)
-
-    def follow(i, carry):
-        @pl.when(i < CHUNKS)
-        def _():
-            total(i)
-
-        to_inner(i - 1).wait_recv()
-        first_pass(pl.ds(pl.multiple_of((i - 1) * width - LANES, LANES), reach), tiles)
-        return carry
-
-    lax.fori_loop(2, CHUNKS + 1, follow, 0)
-    dens[:, last_copy] = dens[:, last_tile]
-    inner_in[:, last_copy] = inner_in[:, last_tile]
-    first_pass(pl.ds(last - LANES, 3 * LANES), 1)
-    first_pass(pl.ds(0, 3 * LANES), 1)
+    first_pass(1, tiles - 2)
+    for i in range(1, CHUNKS - 1):
+        total(i + 1)
+        to_inner(i).wait_recv()
+        first_pass(i * tiles - 1, tiles)
+    to_inner(CHUNKS - 1).wait_recv()
+    first_pass((CHUNKS - 1) * tiles - 1, tiles + 2)
     wrap(flow_x, everything)
+    wrap(dens, near)
     lax.fori_loop(0, n_tiles // FAR_SPAN, finish_far, 0)
     to_pot_far().start()
-    for k in range(2):
-        from_edge(k).wait_recv()
-
-    for t in range(n_tiles // 2):
-        both = edge_in[0, :, at(t)] + edge_in[1, :, at(t)]
-        turned = pltpu.roll(both, 4, 0)
-        outer[:, at(t + 1)] = jnp.where(first_rows, both, turned)
-        outer[:, at(t + 1 + n_tiles // 2)] = jnp.where(first_rows, turned, both)
+    for m in range(2):
+        for k in range(2):
+            from_edge(m, k).wait_recv()
+
+    for m in range(2):
+        for t in range(tiles):
+            both = edge_in[0, :, at(m * tiles + t)] + edge_in[1, :, at(m * tiles + t)]
+            turned = pltpu.roll(both, 4, 0)
+            outer[:, at(2 * m * tiles + t + 1)] = jnp.where(first_rows, both, turned)
+            outer[:, at((2 * m + 1) * tiles + t + 1)] = jnp.where(first_rows, turned, both)
     wrap(outer, everything)
     lax.fori_loop(0, n_tiles // SPAN, second_pass, 0)
     wrap(flow_x, near)
     lax.fori_loop(0, n_tiles // NEAR_SPAN, finish_near, 0)
-    for i in range(CHUNKS):
-        to_core(i).wait_send()
-        to_chip(i).wait_send()
-        to_inner(i).wait_send()
     for i in range(n_tiles // NEAR_SPAN):
-        to_pot(i).wait()
-    to_pot_far().wait()
-    for k in range(2):
-        to_edge(k).wait_send()
+        to_pot(i).wait_recv()
+    to_pot_far().wait_recv()
+    kinds = (
+        edge_in,
+        from_core,
+        from_chip,
+        inner_in.at[:, pl.ds(LANES, cells)],
+        pot_ref.at[near_out, :],
+        pot_ref.at[far_out, :],
+    )
+    for kind, ref in enumerate(kinds):
+        remote(ref, ref, sent.at[kind], edge_recv.at[0], core_peer).wait_send()
 
 
 def apply_kernel(held_ref, pot_ref, applied_ref, out_ref, staged, store_sem, pot_sem):
@@ -529,9 +536,7 @@
             pltpu.SemaphoreType.REGULAR,
             pltpu.SemaphoreType.REGULAR,
         ]
-        + [sems(CHUNKS)] * 6
-        + [sems(2)] * 2
-        + [sems(CHUNKS + 1)] * 2,
+        + [sems(6), sems(CHUNKS), sems(CHUNKS), sems(CHUNKS), sems(4), sems(CHUNKS + 1)],
         compiler_params=pltpu.CompilerParams(
             collective_id=0, has_side_effects=True, vmem_limit_bytes=24 * 1024 * 1024
         ),

time: 23.4 us -> 21.9 us (0.936)
  Pallas kernels: 22.7 us -> 21.2 us
    pallas_call x1, Pallas kernels: 19.1 us -> 17.6 us  [body(): pl.pallas_call(functools.partial(potential_kernel, slabs), out_shape=(plt...]
where the time goes in v6:
time: 21.9 us; the launch traced here: 21.8 us
  Pallas kernels  21.2 us (97%)
  between operations  0.64 us (3%)
    pallas_call x1, Pallas kernels, body(): pl.pallas_call(functools.partial(potential_kernel, slabs), out_shape=(plt...  17.6 us
    pallas_call x1, Pallas kernels, body(): pl.pallas_call(apply_kernel, out_shape=(jax.ShapeDtypeStruct((s_dev, plan...  3.55 us

profile of v6, /device:TPU:1, one launch (start us, length us, event | category | flops | bytes accessed | tf_op | source)
XLA Modules:
  0.0 21.8 jit_solution(9631292883485096779)
XLA Ops:
  0.6 17.6 %potential.1 = (bf16[32,32,4096]{2,1,0:T(8,128)(2,1)S(1)}, f32[32,4096]{1,0:T(8,128)S(1)}) custom-call(s32[32]{0:T(128)} %occ_hbm.1, bf16[32,32,4096]{2,1,0:T(8,128)(2,1)} %states_ref.1, f32[32,4096]{1,0:T(8,128)} %core_ref.1), custom_call_target="tpu_custom_call" | custom-call | tf_op jit(solution)/shard_map/potential/pallas_call | solution.py:510
  18.3 3.6 %apply.1 = (bf16[32,32,4096]{2,1,0:T(8,128)(2,1)}, f32[32,4096]{1,0:T(8,128)}) custom-call(bf16[32,32,4096]{2,1,0:T(8,128)(2,1)S(1)} %get-tuple-element.4.held_ref, f32[32,4096]{1,0:T(8,128)S(1)} %get-tuple-element.5.pot_ref), custom_call_target="tpu_custom_call" | custom-call | tf_op jit(solution)/shard_map/apply/pallas_call | solution.py:545

commit v7 on v6

--- a/solution.py
+++ b/solution.py
@@ -30,9 +30,7 @@
 CHUNKS = 4
 STEP = 4 * LANES
 GATE = 2
-SPAN = 32
-FAR_SPAN = 32
-NEAR_SPAN = 16
+PARTS = ((2, 12), (14, 18), (0, 2))
 STORES = 8
 
 
@@ -118,6 +116,9 @@
     rushed = (slab % 8 == 7) & (upper == 1)
     edge_chips = (chip, 1 - chip)
 
+    near = pl.ds(pl.multiple_of(upper * 8, 8), 8)
+    far = pl.ds(pl.multiple_of((1 - upper) * 8, 8), 8)
+
     def cols(i):
         return pl.ds(pl.multiple_of(i * width, LANES), width)
 
@@ -135,10 +136,10 @@
             part.at[1 - upper, :, cols(i)], from_core.at[:, cols(i)], sent.at[1], core_recv.at[i], core_peer
         )
 
-    def to_chip(i):
-        return remote(
-            chip_sum.at[:, cols(i)], from_chip.at[:, cols(i)], sent.at[2], chip_recv.at[i], chip_peer
-        )
+    def to_chip(rows, i):
+        tile_at = (rows, cols(i))
+        which = i + CHUNKS * (rows is near)
+        return remote(chip_sum.at[tile_at], from_chip.at[tile_at], sent.at[2], chip_recv.at[which], chip_peer)
 
     def edge_cols(m):
         return slice(m * width, (m + 1) * width)
@@ -156,9 +157,8 @@
         return pl.ds(pl.multiple_of(i * width + LANES, LANES), width)
 
     def to_inner(i):
-        rows = pl.ds(pl.multiple_of((1 - upper) * 8, 8), 8)
         return remote(
-            dens.at[rows, shifted(i)], inner_in.at[:, shifted(i)], sent.at[3], inner_recv.at[i], core_peer
+            dens.at[far, shifted(i)], inner_in.at[:, shifted(i)], sent.at[3], inner_recv.at[i], core_peer
         )
 
     def own_rows():
@@ -168,8 +168,8 @@
     far_out = pl.ds(pl.multiple_of(8 + upper * 8, 8), 8)
 
     def to_pot(i):
-        span = NEAR_SPAN * LANES
-        where = pot_ref.at[near_out, pl.ds(pl.multiple_of(i * span, LANES), span)]
+        start, count = PARTS[i]
+        where = pot_ref.at[near_out, pl.ds(start * LANES, count * LANES)]
         return remote(where, where, sent.at[4], pot_recv.at[i], core_peer)
 
     def to_pot_far():
@@ -270,14 +270,17 @@
         @pl.when(jnp.logical_not(rushed))
         def _():
             for i in (2 * m, 2 * m + 1):
-                to_chip(i).start()
+                to_chip(far, i).start()
 
         if m == 1:
 
             @pl.when(rushed)
             def _():
                 for i in range(CHUNKS):
-                    to_chip(i).start()
+                    to_chip(far, i).start()
+
+            for i in range(CHUNKS):
+                to_chip(near, i).start()
 
     for i in range(CHUNKS):
         density_part(1, i)
@@ -327,22 +330,15 @@
     row = lax.broadcasted_iota(jnp.int32, (8, LANES), 0)
     own_four = jnp.where(is_low, row, 7 - row) < 4
     own_two = jnp.where(is_low, row, 7 - row) < 2
-    near = pl.ds(pl.multiple_of(upper * 8, 8), 8)
-    far = pl.ds(pl.multiple_of((1 - upper) * 8, 8), 8)
 
     tiles = width // LANES
-    reach = (tiles + 2) * LANES
-    last = n_tiles * LANES
-    first_copy, last_copy = slice(last + LANES, last + 2 * LANES), slice(0, LANES)
-    first_tile, last_tile = slice(LANES, 2 * LANES), slice(last, last + LANES)
 
     def at(j):
         return slice(j * LANES, (j + 1) * LANES)
 
-    def total(i):
-        to_chip(i).wait_recv()
-        dens[:, shifted(i)] = chip_sum[:, cols(i)] + from_chip[:, cols(i)]
-        to_inner(i).start()
+    def total(rows, i):
+        to_chip(rows, i).wait_recv()
+        dens[rows, shifted(i)] = chip_sum[rows, cols(i)] + from_chip[rows, cols(i)]
 
     def flows(fields, turned, j):
         centre = fields[j]
@@ -373,19 +369,15 @@
             near_rest[:, where[j]] = jnp.where(is_low, rest[:8], rest[8:])
             near_z[:, where[j]] = jnp.where(is_low, part_z[:8], part_z[8:half])
 
-    def second_pass(g, carry):
-        where = pl.ds(pl.multiple_of(g * SPAN * LANES, LANES), (SPAN + 2) * LANES)
-        dens_w, flow_w, local_w = (ref.at[near, where] for ref in (dens, flow_x, local))
-        outer_w, rest_w, z_w = (ref.at[:, where] for ref in (outer, near_rest, near_z))
-        fields = [
-            jnp.where(own_four, outer_w[:, at(j)], pltpu.roll(dens_w[:, at(j)], 4, 0)) for j in range(SPAN + 2)
-        ]
+    def second_pass(start, count):
+        where = [at(t % n_tiles + 1) for t in range(start - 1, start + count + 1)]
+        fields = [jnp.where(own_four, outer[:, w], pltpu.roll(dens[near, w], 4, 0)) for w in where]
         turned = [swap_halves(f) for f in fields]
-        for j in range(1, SPAN + 1):
+        for j in range(1, count + 1):
             part_x, part_y, part_z, d_dens = flows(fields, turned, j)
             rest = d_dens - along_y(part_y, swap_halves(part_y), inner)
-            rest = jnp.where(own_two, pltpu.roll(rest, 4, 0), rest_w[:, at(j)])
-            old_z = z_w[:, at(j)]
+            rest = jnp.where(own_two, pltpu.roll(rest, 4, 0), near_rest[:, where[j]])
+            old_z = near_z[:, where[j]]
             row_z = jnp.where(
                 first_rows,
                 pltpu.roll(jnp.where(is_low, part_z, old_z), 6, 0),
@@ -393,63 +385,50 @@
             )
             div_z = along_z(row_z)
             div_z = jnp.where(is_low, pltpu.roll(div_z, 6, 0), pltpu.roll(div_z, 2, 0))
-            local_w[:, at(j)] = jnp.where(own_four, rest - div_z, local_w[:, at(j)])
-            flow_w[:, at(j)] = jnp.where(own_two, pltpu.roll(part_x, 4, 0), flow_w[:, at(j)])
-        return carry
-
-    def finish(rows, out_rows, g, span):
-        where = pl.ds(pl.multiple_of(g * span * LANES, LANES), (span + 2) * LANES)
-        flow_w, local_w = flow_x.at[rows, where], local.at[rows, where]
-        out_w = pot_ref.at[out_rows, pl.ds(pl.multiple_of(g * span * LANES, LANES), span * LANES)]
-        fields = [flow_w[:, at(j)] for j in range(span + 2)]
+            local[near, where[j]] = jnp.where(own_four, rest - div_z, local[near, where[j]])
+            flow_x[near, where[j]] = jnp.where(own_two, pltpu.roll(part_x, 4, 0), flow_x[near, where[j]])
+
+    def finish(rows, out_rows, start, count):
+        where = [at(t % n_tiles + 1) for t in range(start - 1, start + count + 1)]
+        fields = [flow_x[rows, w] for w in where]
         turned = [swap_halves(f) for f in fields]
-        for j in range(1, span + 1):
+        for j in range(1, count + 1):
             div_x = along_x(fields[j - 1], turned[j - 1], turned[j], fields[j + 1], turned[j + 1], low)
-            out_w[:, at(j - 1)] = local_w[:, at(j)] - div_x
-
-    def finish_far(g, carry):
-        finish(far, far_out, g, FAR_SPAN)
-        return carry
-
-    def finish_near(g, carry):
-        finish(near, near_out, g, NEAR_SPAN)
-        to_pot(g).start()
-        return carry
-
-    def wrap(ref, rows):
-        ref[rows, first_copy] = ref[rows, first_tile]
-        ref[rows, last_copy] = ref[rows, last_tile]
-
-    everything = slice(None)
-    total(0)
-    total(1)
-    to_inner(0).wait_recv()
-    first_pass(1, tiles - 2)
-    for i in range(1, CHUNKS - 1):
-        total(i + 1)
-        to_inner(i).wait_recv()
-        first_pass(i * tiles - 1, tiles)
-    to_inner(CHUNKS - 1).wait_recv()
-    first_pass((CHUNKS - 1) * tiles - 1, tiles + 2)
-    wrap(flow_x, everything)
-    wrap(dens, near)
-    lax.fori_loop(0, n_tiles // FAR_SPAN, finish_far, 0)
-    to_pot_far().start()
-    for m in range(2):
+            pot_ref[out_rows, at((start + j - 1) % n_tiles)] = local[rows, where[j]] - div_x
+
+    def unpack(m):
         for k in range(2):
             from_edge(m, k).wait_recv()
-
-    for m in range(2):
         for t in range(tiles):
             both = edge_in[0, :, at(m * tiles + t)] + edge_in[1, :, at(m * tiles + t)]
             turned = pltpu.roll(both, 4, 0)
             outer[:, at(2 * m * tiles + t + 1)] = jnp.where(first_rows, both, turned)
             outer[:, at((2 * m + 1) * tiles + t + 1)] = jnp.where(first_rows, turned, both)
-    wrap(outer, everything)
-    lax.fori_loop(0, n_tiles // SPAN, second_pass, 0)
-    wrap(flow_x, near)
-    lax.fori_loop(0, n_tiles // NEAR_SPAN, finish_near, 0)
-    for i in range(n_tiles // NEAR_SPAN):
+
+    for i in range(CHUNKS):
+        total(far, i)
+        to_inner(i).start()
+    for i in range(CHUNKS):
+        total(near, i)
+        to_inner(i).wait_recv()
+        if i == 0:
+            first_pass(1, tiles - 2)
+        elif i < CHUNKS - 1:
+            first_pass(i * tiles - 1, tiles)
+        else:
+            first_pass(i * tiles - 1, tiles + 2)
+    finish(far, far_out, 0, n_tiles)
+    to_pot_far().start()
+    unpack(0)
+    second_pass(1, 2 * tiles - 2)
+    finish(near, near_out, *PARTS[0])
+    to_pot(0).start()
+    unpack(1)
+    second_pass(2 * tiles - 1, 2 * tiles + 2)
+    for i in (1, 2):
+        finish(near, near_out, *PARTS[i])
+        to_pot(i).start()
+    for i in range(len(PARTS)):
         to_pot(i).wait_recv()
     to_pot_far().wait_recv()
     kinds = (
@@ -536,7 +515,7 @@
             pltpu.SemaphoreType.REGULAR,
             pltpu.SemaphoreType.REGULAR,
         ]
-        + [sems(6), sems(CHUNKS), sems(CHUNKS), sems(CHUNKS), sems(4), sems(CHUNKS + 1)],
+        + [sems(6), sems(CHUNKS), sems(2 * CHUNKS), sems(CHUNKS), sems(4), sems(CHUNKS + 1)],
         compiler_params=pltpu.CompilerParams(
             collective_id=0, has_side_effects=True, vmem_limit_bytes=24 * 1024 * 1024
         ),

time: 21.9 us -> 21.6 us (0.986)
  Pallas kernels: 21.2 us -> 20.9 us
    pallas_call x1, Pallas kernels: 17.6 us -> 17.3 us  [body(): pl.pallas_call(functools.partial(potential_kernel, slabs), out_shape=(plt...]
where the time goes in v7:
time: 21.6 us; the launch traced here: 21.5 us
  Pallas kernels  20.9 us (97%)
  between operations  0.64 us (3%)
    pallas_call x1, Pallas kernels, body(): pl.pallas_call(functools.partial(potential_kernel, slabs), out_shape=(plt...  17.3 us
    pallas_call x1, Pallas kernels, body(): pl.pallas_call(apply_kernel, out_shape=(jax.ShapeDtypeStruct((s_dev, plan...  3.55 us

profile of v7, /device:TPU:1, one launch (start us, length us, event | category | flops | bytes accessed | tf_op | source)
XLA Modules:
  0.0 21.5 jit_solution(16785910122709636955)
XLA Ops:
  0.6 17.3 %potential.1 = (bf16[32,32,4096]{2,1,0:T(8,128)(2,1)S(1)}, f32[32,4096]{1,0:T(8,128)S(1)}) custom-call(s32[32]{0:T(128)} %occ_hbm.1, bf16[32,32,4096]{2,1,0:T(8,128)(2,1)} %states_ref.1, f32[32,4096]{1,0:T(8,128)} %core_ref.1), custom_call_target="tpu_custom_call" | custom-call | tf_op jit(solution)/shard_map/potential/pallas_call | solution.py:489
  18.0 3.6 %apply.1 = (bf16[32,32,4096]{2,1,0:T(8,128)(2,1)}, f32[32,4096]{1,0:T(8,128)}) custom-call(bf16[32,32,4096]{2,1,0:T(8,128)(2,1)S(1)} %get-tuple-element.4.held_ref, f32[32,4096]{1,0:T(8,128)S(1)} %get-tuple-element.5.pot_ref), custom_call_target="tpu_custom_call" | custom-call | tf_op jit(solution)/shard_map/apply/pallas_call | solution.py:524

commit v8 on v7

--- a/solution.py
+++ b/solution.py
@@ -29,6 +29,7 @@
 
 CHUNKS = 4
 STEP = 4 * LANES
+LOADS = 8
 GATE = 2
 PARTS = ((2, 12), (14, 18), (0, 2))
 STORES = 8
@@ -114,7 +115,7 @@
     beyond = (slab + slabs - 1 + 2 * upper) % slabs
     wrapped = slab % 8 == 0
     rushed = (slab % 8 == 7) & (upper == 1)
-    edge_chips = (chip, 1 - chip)
+    edge_chips = (0, 1)
 
     near = pl.ds(pl.multiple_of(upper * 8, 8), 8)
     far = pl.ds(pl.multiple_of((1 - upper) * 8, 8), 8)
@@ -123,8 +124,8 @@
         return pl.ds(pl.multiple_of(i * width, LANES), width)
 
     def load(h, i):
-        where = (slice(None), pl.ds(h * half, half), cols(i))
-        return pltpu.make_async_copy(states_ref.at[where], held_ref.at[where], load_sem.at[h * CHUNKS + i])
+        where = (slice(None), pl.ds(h * half, half), pl.ds(pl.multiple_of(i * STEP, STEP), STEP))
+        return pltpu.make_async_copy(states_ref.at[where], held_ref.at[where], load_sem.at[h * LOADS + i])
 
     def remote(src, dst, send, recv, peer):
         return pltpu.make_async_remote_copy(
@@ -133,13 +134,13 @@
 
     def to_core(i):
         return remote(
-            part.at[1 - upper, :, cols(i)], from_core.at[:, cols(i)], sent.at[1], core_recv.at[i], core_peer
+            part.at[1 - upper, :, cols(i)], from_core.at[:, cols(i)], sent.at[0], core_recv.at[i], core_peer
         )
 
     def to_chip(rows, i):
         tile_at = (rows, cols(i))
         which = i + CHUNKS * (rows is near)
-        return remote(chip_sum.at[tile_at], from_chip.at[tile_at], sent.at[2], chip_recv.at[which], chip_peer)
+        return remote(chip_sum.at[tile_at], from_chip.at[tile_at], sent.at[0], chip_recv.at[which], chip_peer)
 
     def edge_cols(m):
         return slice(m * width, (m + 1) * width)
@@ -147,18 +148,18 @@
     def to_edge(m, k):
         peer = {"grp": edge_chips[k] * 2 + upper, "slab": beyond}
         out = edge_out.at[:, edge_cols(m)]
-        return remote(out, edge_in.at[chip, :, edge_cols(m)], sent.at[0], edge_recv.at[2 * m + chip], peer)
+        return remote(out, edge_in.at[chip, :, edge_cols(m)], sent.at[1], edge_recv.at[2 * m + chip], peer)
 
     def from_edge(m, k):
         out = edge_out.at[:, edge_cols(m)]
-        return remote(out, edge_in.at[k, :, edge_cols(m)], sent.at[0], edge_recv.at[2 * m + k], core_peer)
+        return remote(out, edge_in.at[k, :, edge_cols(m)], sent.at[1], edge_recv.at[2 * m + k], core_peer)
 
     def shifted(i):
         return pl.ds(pl.multiple_of(i * width + LANES, LANES), width)
 
     def to_inner(i):
         return remote(
-            dens.at[far, shifted(i)], inner_in.at[:, shifted(i)], sent.at[3], inner_recv.at[i], core_peer
+            dens.at[far, shifted(i)], inner_in.at[:, shifted(i)], sent.at[1], inner_recv.at[i], core_peer
         )
 
     def own_rows():
@@ -170,11 +171,11 @@
     def to_pot(i):
         start, count = PARTS[i]
         where = pot_ref.at[near_out, pl.ds(start * LANES, count * LANES)]
-        return remote(where, where, sent.at[4], pot_recv.at[i], core_peer)
+        return remote(where, where, sent.at[1], pot_recv.at[i], core_peer)
 
     def to_pot_far():
         where = pot_ref.at[far_out, :]
-        return remote(where, where, sent.at[5], pot_recv.at[CHUNKS], core_peer)
+        return remote(where, where, sent.at[1], pot_recv.at[len(PARTS)], core_peer)
 
     barrier = pltpu.get_barrier_semaphore()
 
@@ -196,11 +197,11 @@
 
     occ_copy = pltpu.make_async_copy(occ_hbm, occ_ref, misc_sem.at[0])
     occ_copy.start()
-    for i in range(CHUNKS):
+    for i in range(LOADS):
         load(1, i).start()
     core_copy = pltpu.make_async_copy(core_ref.at[own_rows(), :], core_half, misc_sem.at[1])
     core_copy.start()
-    for i in range(CHUNKS):
+    for i in range(LOADS):
         load(0, i).start()
 
     occ_copy.wait()
@@ -210,9 +211,8 @@
     ]
 
     def density_part(h, i):
-        load(h, i).wait()
-
         def tile_step(t, carry):
+            load(h, i * (width // STEP) + t).wait()
             lanes = pl.ds(pl.multiple_of(i * width + t * STEP, STEP), STEP)
             total = jnp.zeros((half, STEP), jnp.float32)
             for s in range(s_dev):
@@ -301,12 +301,12 @@
 
     core_copy.wait()
     for i in range(CHUNKS):
-        if i % 2 == 0:
+        if i < 2:
             @pl.when(upper == 1)
             def _():
                 if i == 0:
                     pl.semaphore_wait(group_sem, 1)
-                sum_and_send(i // 2)
+                sum_and_send(i)
         density_part(0, i)
 
         @pl.when(upper == 1)
@@ -431,16 +431,8 @@
     for i in range(len(PARTS)):
         to_pot(i).wait_recv()
     to_pot_far().wait_recv()
-    kinds = (
-        edge_in,
-        from_core,
-        from_chip,
-        inner_in.at[:, pl.ds(LANES, cells)],
-        pot_ref.at[near_out, :],
-        pot_ref.at[far_out, :],
-    )
-    for kind, ref in enumerate(kinds):
-        remote(ref, ref, sent.at[kind], edge_recv.at[0], core_peer).wait_send()
+    for k in range(2):
+        remote(part, part, sent.at[k], edge_recv.at[0], core_peer).wait_send()
 
 
 def apply_kernel(held_ref, pot_ref, applied_ref, out_ref, staged, store_sem, pot_sem):
@@ -510,12 +502,12 @@
             wide(half),
             wide(8),
             wide(8),
-            sems(2 * CHUNKS),
+            sems(2 * LOADS),
             sems(2),
             pltpu.SemaphoreType.REGULAR,
             pltpu.SemaphoreType.REGULAR,
         ]
-        + [sems(6), sems(CHUNKS), sems(2 * CHUNKS), sems(CHUNKS), sems(4), sems(CHUNKS + 1)],
+        + [sems(2), sems(CHUNKS), sems(2 * CHUNKS), sems(CHUNKS), sems(4), sems(len(PARTS) + 1)],
         compiler_params=pltpu.CompilerParams(
             collective_id=0, has_side_effects=True, vmem_limit_bytes=24 * 1024 * 1024
         ),

time: 21.6 us -> 21.4 us (level)
  no operation moved by 1% of the time
where the time goes in v8:
time: 21.4 us; the launch traced here: 21.3 us
  Pallas kernels  20.7 us (97%)
  between operations  0.64 us (3%)
    pallas_call x1, Pallas kernels, body(): pl.pallas_call(functools.partial(potential_kernel, slabs), out_shape=(plt...  17.1 us
    pallas_call x1, Pallas kernels, body(): pl.pallas_call(apply_kernel, out_shape=(jax.ShapeDtypeStruct((s_dev, plan...  3.55 us

profile of v8, /device:TPU:1, one launch (start us, length us, event | category | flops | bytes accessed | tf_op | source)
XLA Modules:
  0.0 21.3 jit_solution(9728500897826990306)
XLA Ops:
  0.6 17.1 %potential.1 = (bf16[32,32,4096]{2,1,0:T(8,128)(2,1)S(1)}, f32[32,4096]{1,0:T(8,128)S(1)}) custom-call(s32[32]{0:T(128)} %occ_hbm.1, bf16[32,32,4096]{2,1,0:T(8,128)(2,1)} %states_ref.1, f32[32,4096]{1,0:T(8,128)} %core_ref.1), custom_call_target="tpu_custom_call" | custom-call | tf_op jit(solution)/shard_map/potential/pallas_call | solution.py:481
  17.8 3.6 %apply.1 = (bf16[32,32,4096]{2,1,0:T(8,128)(2,1)}, f32[32,4096]{1,0:T(8,128)}) custom-call(bf16[32,32,4096]{2,1,0:T(8,128)(2,1)S(1)} %get-tuple-element.4.held_ref, f32[32,4096]{1,0:T(8,128)S(1)} %get-tuple-element.5.pot_ref), custom_call_target="tpu_custom_call" | custom-call | tf_op jit(solution)/shard_map/apply/pallas_call | solution.py:516

commit v9 on v8

--- a/solution.py
+++ b/solution.py
@@ -30,7 +30,7 @@
 CHUNKS = 4
 STEP = 4 * LANES
 LOADS = 8
-GATE = 2
+GATE = 1
 PARTS = ((2, 12), (14, 18), (0, 2))
 STORES = 8
 
@@ -301,12 +301,12 @@
 
     core_copy.wait()
     for i in range(CHUNKS):
-        if i < 2:
+        if i == 0:
             @pl.when(upper == 1)
             def _():
-                if i == 0:
-                    pl.semaphore_wait(group_sem, 1)
-                sum_and_send(i)
+                pl.semaphore_wait(group_sem, 1)
+                for m in range(2):
+                    sum_and_send(m)
         density_part(0, i)
 
         @pl.when(upper == 1)

time: 21.4 us -> 21.1 us (0.986)
  Pallas kernels: 20.7 us -> 20.3 us
    pallas_call x1, Pallas kernels: 17.1 us -> 16.8 us  [body(): pl.pallas_call(functools.partial(potential_kernel, slabs), out_shape=(plt...]
where the time goes in v9:
time: 21.1 us; the launch traced here: 21 us
  Pallas kernels  20.3 us (96%)
  between operations  0.64 us (3%)
    pallas_call x1, Pallas kernels, body(): pl.pallas_call(functools.partial(potential_kernel, slabs), out_shape=(plt...  16.8 us
    pallas_call x1, Pallas kernels, body(): pl.pallas_call(apply_kernel, out_shape=(jax.ShapeDtypeStruct((s_dev, plan...  3.55 us

profile of v9, /device:TPU:1, one launch (start us, length us, event | category | flops | bytes accessed | tf_op | source)
XLA Modules:
  0.0 21.0 jit_solution(18018097674896457938)
XLA Ops:
  0.6 16.8 %potential.1 = (bf16[32,32,4096]{2,1,0:T(8,128)(2,1)S(1)}, f32[32,4096]{1,0:T(8,128)S(1)}) custom-call(s32[32]{0:T(128)} %occ_hbm.1, bf16[32,32,4096]{2,1,0:T(8,128)(2,1)} %states_ref.1, f32[32,4096]{1,0:T(8,128)} %core_ref.1), custom_call_target="tpu_custom_call" | custom-call | tf_op jit(solution)/shard_map/potential/pallas_call | solution.py:481
  17.4 3.6 %apply.1 = (bf16[32,32,4096]{2,1,0:T(8,128)(2,1)}, f32[32,4096]{1,0:T(8,128)}) custom-call(bf16[32,32,4096]{2,1,0:T(8,128)(2,1)S(1)} %get-tuple-element.4.held_ref, f32[32,4096]{1,0:T(8,128)S(1)} %get-tuple-element.5.pot_ref), custom_call_target="tpu_custom_call" | custom-call | tf_op jit(solution)/shard_map/apply/pallas_call | solution.py:516

commit v10 on v9

--- a/solution.py
+++ b/solution.py
@@ -124,8 +124,9 @@
         return pl.ds(pl.multiple_of(i * width, LANES), width)
 
     def load(h, i):
-        where = (slice(None), pl.ds(h * half, half), pl.ds(pl.multiple_of(i * STEP, STEP), STEP))
-        return pltpu.make_async_copy(states_ref.at[where], held_ref.at[where], load_sem.at[h * LOADS + i])
+        span = STEP if h == 1 else width
+        where = (slice(None), pl.ds(h * half, half), pl.ds(pl.multiple_of(i * span, STEP), span))
+        return pltpu.make_async_copy(states_ref.at[where], held_ref.at[where], load_sem.at[h * CHUNKS + i])
 
     def remote(src, dst, send, recv, peer):
         return pltpu.make_async_remote_copy(
@@ -201,7 +202,7 @@
         load(1, i).start()
     core_copy = pltpu.make_async_copy(core_ref.at[own_rows(), :], core_half, misc_sem.at[1])
     core_copy.start()
-    for i in range(LOADS):
+    for i in range(CHUNKS):
         load(0, i).start()
 
     occ_copy.wait()
@@ -211,8 +212,12 @@
     ]
 
     def density_part(h, i):
+        if h == 0:
+            load(0, i).wait()
+
         def tile_step(t, carry):
-            load(h, i * (width // STEP) + t).wait()
+            if h == 1:
+                load(1, i * (width // STEP) + t).wait()
             lanes = pl.ds(pl.multiple_of(i * width + t * STEP, STEP), STEP)
             total = jnp.zeros((half, STEP), jnp.float32)
             for s in range(s_dev):
@@ -425,8 +430,8 @@
     to_pot(0).start()
     unpack(1)
     second_pass(2 * tiles - 1, 2 * tiles + 2)
+    finish(near, near_out, PARTS[1][0], PARTS[1][1] + PARTS[2][1])
     for i in (1, 2):
-        finish(near, near_out, *PARTS[i])
         to_pot(i).start()
     for i in range(len(PARTS)):
         to_pot(i).wait_recv()
@@ -502,7 +507,7 @@
             wide(half),
             wide(8),
             wide(8),
-            sems(2 * LOADS),
+            sems(LOADS + CHUNKS),
             sems(2),
             pltpu.SemaphoreType.REGULAR,
             pltpu.SemaphoreType.REGULAR,

time: 21.1 us -> 21.1 us (level)
  no operation moved by 1% of the time
where the time goes in v10:
time: 21.1 us; the launch traced here: 20.9 us
  Pallas kernels  20.3 us (96%)
  between operations  0.64 us (3%)
    pallas_call x1, Pallas kernels, body(): pl.pallas_call(functools.partial(potential_kernel, slabs), out_shape=(plt...  16.8 us
    pallas_call x1, Pallas kernels, body(): pl.pallas_call(apply_kernel, out_shape=(jax.ShapeDtypeStruct((s_dev, plan...  3.55 us

profile of v10, /device:TPU:1, one launch (start us, length us, event | category | flops | bytes accessed | tf_op | source)
XLA Modules:
  0.0 20.9 jit_solution(16985119465900716190)
XLA Ops:
  0.6 16.8 %potential.1 = (bf16[32,32,4096]{2,1,0:T(8,128)(2,1)S(1)}, f32[32,4096]{1,0:T(8,128)S(1)}) custom-call(s32[32]{0:T(128)} %occ_hbm.1, bf16[32,32,4096]{2,1,0:T(8,128)(2,1)} %states_ref.1, f32[32,4096]{1,0:T(8,128)} %core_ref.1), custom_call_target="tpu_custom_call" | custom-call | tf_op jit(solution)/shard_map/potential/pallas_call | solution.py:486
  17.4 3.6 %apply.1 = (bf16[32,32,4096]{2,1,0:T(8,128)(2,1)}, f32[32,4096]{1,0:T(8,128)}) custom-call(bf16[32,32,4096]{2,1,0:T(8,128)(2,1)S(1)} %get-tuple-element.4.held_ref, f32[32,4096]{1,0:T(8,128)S(1)} %get-tuple-element.5.pot_ref), custom_call_target="tpu_custom_call" | custom-call | tf_op jit(solution)/shard_map/apply/pallas_call | solution.py:521

commit v11 on v10

--- a/solution.py
+++ b/solution.py
@@ -32,7 +32,7 @@
 LOADS = 8
 GATE = 1
 PARTS = ((2, 12), (14, 18), (0, 2))
-STORES = 8
+STORES = 4
 
 
 def stencil(before2, before1, after1, after2):

time: 21.1 us -> 21.1 us (level)
  no operation moved by 1% of the time
where the time goes in v11:
time: 21.1 us; the launch traced here: 20.9 us
  Pallas kernels  20.3 us (96%)
  between operations  0.64 us (3%)
    pallas_call x1, Pallas kernels, body(): pl.pallas_call(functools.partial(potential_kernel, slabs), out_shape=(plt...  16.8 us
    pallas_call x1, Pallas kernels, body(): pl.pallas_call(apply_kernel, out_shape=(jax.ShapeDtypeStruct((s_dev, plan...  3.55 us

profile of v11, /device:TPU:1, one launch (start us, length us, event | category | flops | bytes accessed | tf_op | source)
XLA Modules:
  0.0 20.9 jit_solution(12329581171376588715)
XLA Ops:
  0.6 16.8 %potential.1 = (bf16[32,32,4096]{2,1,0:T(8,128)(2,1)S(1)}, f32[32,4096]{1,0:T(8,128)S(1)}) custom-call(s32[32]{0:T(128)} %occ_hbm.1, bf16[32,32,4096]{2,1,0:T(8,128)(2,1)} %states_ref.1, f32[32,4096]{1,0:T(8,128)} %core_ref.1), custom_call_target="tpu_custom_call" | custom-call | tf_op jit(solution)/shard_map/potential/pallas_call | solution.py:486
  17.4 3.5 %apply.1 = (bf16[32,32,4096]{2,1,0:T(8,128)(2,1)}, f32[32,4096]{1,0:T(8,128)}) custom-call(bf16[32,32,4096]{2,1,0:T(8,128)(2,1)S(1)} %get-tuple-element.4.held_ref, f32[32,4096]{1,0:T(8,128)S(1)} %get-tuple-element.5.pot_ref), custom_call_target="tpu_custom_call" | custom-call | tf_op jit(solution)/shard_map/apply/pallas_call | solution.py:521
